TPU v7x, 32 devices: a whole 2x2x4 slice. The times are simulated.
32 devices in a mesh: grp: 2 (over x), band: 16 (over z, y, core).
Axes of the slice: x: 2, y: 2, z: 4, core: 2. Of those that a mesh axis runs over, the one named last changes fastest.
Arguments:
- source_field: bfloat16 [1024, 128, 256], P(('grp', 'band')), parts along dimension 0, may hold values from -6 to 6
- interp_weight: bfloat16 [1536, 128, 128], P('band'), may hold values from -0.5 to 0.5
- dest_band: int32 [1536, 1], P('band'), may hold values from 0 to 15; in each aligned block of 96 rows (0 to 95, 96 to 191, ...) at most 9 rows name the same one
- target_block: int32 [1536], P('band'), may hold values from 0 to 44
- source_block: int32 [1536], P('band'), may hold values from 0 to 31
- entry_count: int32 [16], P('band'), may hold values from 1 to 96, 1152 in all
- mode_index: int32 [384], replicated, may hold values from 0 to 720, as said below
- filter_weight: bfloat16 [64, 2, 384, 256], P(None, None, 'band'), may hold values from -4 to 4
Outputs:
- processed: bfloat16 [184320, 256], P(('grp', 'band')), parts along dimension 0
There are 2 independent parts, one for each index of `grp`. A program takes and returns all parts, laid end to end along the dimension named above; an argument that names none is the same for every part. Nothing has to cross between parts.
Inputs may be any that keep to these rules, and one draw needn't show every extreme that they name: `dest_band`: among the entries of one device no band is named more than 9 times, a bound that some block reaches. `entry_count`: the counts sum to 1152; entries of a device past its count are padding. `mode_index`: distinct wavenumbers; 0 and 720 are always among them.
All inputs are finite; a program needn't handle non-finite values.
Results may differ from a plain program's by a relative error of at most 0.0076.
Values may be sent and summed in bfloat16 or wider, within the bound.
A program may use at most 128 MiB of HBM per device.

v0:
```python
import math

import jax
import jax.numpy as jnp
from jax import lax
from jax.sharding import PartitionSpec as P

NLON = 1440
LAT_DEV = 4
TB_DEV = 45


def lon_tables(mode_index):
    grid_n = jnp.arange(NLON, dtype=jnp.int32)
    phase = grid_n[:, None] * mode_index[None, :] % NLON
    angle = phase.astype(jnp.float32) * (2.0 * math.pi / NLON)
    forward = jnp.concatenate([jnp.cos(angle), -jnp.sin(angle)], axis=1).astype(jnp.bfloat16)
    factor = jnp.where((mode_index == 0) | (mode_index == NLON // 2), 1.0, 2.0).astype(jnp.float32)
    inverse = jnp.concatenate(
        [factor[None, :] * jnp.cos(angle), -factor[None, :] * jnp.sin(angle)], axis=1
    )
    return (forward, inverse.T.astype(jnp.bfloat16))


def lat_table(nlat):
    index = jnp.arange(nlat, dtype=jnp.int32)
    phase = index[:, None] * index[None, :] % nlat
    angle = phase.astype(jnp.float32) * (2.0 * math.pi / nlat)
    cosine = jnp.cos(angle)
    sine = jnp.sin(angle)
    upper = jnp.stack([cosine, sine], axis=2)
    lower = jnp.stack([-sine, cosine], axis=2)
    table = jnp.stack([upper, lower], axis=1)
    return table.reshape(2 * nlat, 2 * nlat).astype(jnp.bfloat16)


def per_device(
    source_field,
    interp_weight,
    dest_band,
    target_block,
    source_block,
    entry_count,
    mode_index,
    filter_weight,
):
    bands = lax.axis_size("band")
    entries = interp_weight.shape[0]
    slots = max(2, 3 * entries // (2 * bands))
    total_slots = bands * slots
    pixels = source_field.shape[1]
    channels = source_field.shape[2]
    modes = mode_index.shape[0]
    dest = dest_band[:, 0]
    valid = jnp.arange(entries, dtype=jnp.int32) < entry_count[0]
    hits = (dest[:, None] == jnp.arange(bands, dtype=jnp.int32)[None, :]).astype(jnp.int32)
    before = jnp.cumsum(hits, axis=0) - hits
    rank = jnp.sum(before * hits, axis=1)
    position = dest * slots + rank
    target_ids = (
        jnp.zeros((total_slots,), jnp.int32).at[position].set(target_block).reshape(bands, slots)
    )
    picked = jnp.take(source_field, source_block, axis=0)
    made = jnp.einsum("eij,ejc->eic", interp_weight, picked, preferred_element_type=jnp.float32)
    made = (made * valid.astype(jnp.float32)[:, None, None]).astype(jnp.bfloat16)
    sending = jnp.zeros((total_slots, pixels, channels), jnp.bfloat16).at[position].set(made)
    sending = sending.reshape(bands, slots, pixels, channels)
    arrived, arrived_ids = (
        lax.all_to_all(sending, "band", split_axis=0, concat_axis=0, tiled=True),
        lax.all_to_all(target_ids, "band", split_axis=0, concat_axis=0, tiled=True),
    )
    flat_ids = arrived_ids.reshape(total_slots)
    picker = (jnp.arange(TB_DEV, dtype=jnp.int32)[:, None] == flat_ids[None, :]).astype(
        jnp.bfloat16
    )
    summed = jnp.dot(
        picker, arrived.reshape(total_slots, pixels * channels), preferred_element_type=jnp.float32
    )
    regridded = summed.astype(jnp.bfloat16).reshape(LAT_DEV, NLON, channels)
    forward, inverse = lon_tables(mode_index)
    spectrum = jnp.einsum("lnc,nk->lkc", regridded, forward, preferred_element_type=jnp.float32) * (
        1.0 / math.sqrt(NLON)
    )
    spectrum = spectrum.astype(jnp.bfloat16).reshape(LAT_DEV, 2, modes, channels)
    pencils = lax.all_to_all(spectrum, "band", split_axis=2, concat_axis=0, tiled=True)
    nlat = pencils.shape[0]
    mode_dev = pencils.shape[2]
    table = lat_table(nlat)
    mixed = jnp.dot(
        table, pencils.reshape(2 * nlat, mode_dev * channels), preferred_element_type=jnp.float32
    ) * (1.0 / math.sqrt(nlat))
    mixed = mixed.reshape(nlat, 2, mode_dev, channels)
    filt = filter_weight.astype(jnp.float32)
    real_part = filt[:, 0] * mixed[:, 0] - filt[:, 1] * mixed[:, 1]
    imag_part = filt[:, 0] * mixed[:, 1] + filt[:, 1] * mixed[:, 0]
    shaped = (
        jnp.stack([real_part, imag_part], axis=1)
        .astype(jnp.bfloat16)
        .reshape(2 * nlat, mode_dev * channels)
    )
    back = lax.dot_general(
        table, shaped, (((0,), (0,)), ((), ())), preferred_element_type=jnp.float32
    ) * (1.0 / math.sqrt(nlat))
    back = back.astype(jnp.bfloat16).reshape(nlat, 2, mode_dev, channels)
    returned = lax.all_to_all(back, "band", split_axis=0, concat_axis=2, tiled=True)
    filtered = jnp.einsum(
        "lkc,kn->lnc",
        returned.reshape(LAT_DEV, 2 * modes, channels),
        inverse,
        preferred_element_type=jnp.float32,
    ) * (1.0 / math.sqrt(NLON))
    processed = (regridded.astype(jnp.float32) + filtered).astype(jnp.bfloat16)
    return processed.reshape(LAT_DEV * NLON, channels)


def solution(mesh):
    in_specs = (
        P(("grp", "band"), None, None),
        P("band", None, None),
        P("band", None),
        P("band"),
        P("band"),
        P("band"),
        P(),
        P(None, None, "band", None),
    )
    out_specs = P(("grp", "band"), None)
    return jax.shard_map(
        per_device, mesh=mesh, in_specs=in_specs, out_specs=out_specs, check_vma=False
    )
```

profile of v0, /device:TPU:1, one launch (start us, length us, event | category | flops | bytes accessed | tf_op | source)
XLA Modules:
  0.0 397.9 jit_solution(1304532199287910457)
XLA Ops:
  0.0 0.9 fusion.22
  0.9 0.1 reduce_window_sum.11
  1.0 0.8 select_reduce_fusion
  1.9 0.7 fusion.32
  2.5 1.0 scatter_custom_fusion
  3.5 0.7 all_to_all.31
  4.2 7.3 %all-to-all-start = ((s32[16,1,9]{2,1,0:T(1,128)}), s32[16,1,9]{2,1,0:T(1,128)S(1)}, u32[]{:S(2)}, u32[]{:S(2)}) async-start(s32[16,1,9]{2,1,0:T(1,128)} %bitcast.3), calls=%async_computation | async-start | bytes 16384 | tf_op jit(solution)/shard_map/all_to_all | solution.py:70
  12.2 0.7 compare_select_fusion
  12.9 0.7 compare_convert_fusion
  13.6 7.6 %gather_fusion = bf16[96,128,256]{2,1,0:T(8,128)(2,1)} fusion(bf16[32,128,256]{2,1,0:T(8,128)(2,1)} %param.8, s32[1024]{0:T(1024)S(1)} %pad_clamp_fusion), kind=kCustom, calls=%fused_computation | custom fusion | bytes 12583296 | tf_op jit(solution)/shard_map/jit(_take)/gather | solution.py:63
  21.1 8.3 %fusion.1 = bf16[96,128,256]{1,2,0:T(8,128)(2,1)} fusion(f32[96]{0:T(128)S(1)} %get-tuple-element.15, bf16[96,128,128]{2,1,0:T(8,128)(2,1)S(1)} %copy-done, bf16[96,128,256]{2,1,0:T(8,128)(2,1)} %gather_fusion, pred[96]{0:T(512)(128)(4,1)S(1)} %get-tuple-element.16), kind=kOutput, calls=%fused_computation.8 | convolution fusion | flops 814743552 | bytes 15729120 | tf_op jit(solution)/shard_map/eij,ejc->eic/dot_general | solution.py:64
  29.4 8.6 %copy.23 = bf16[96,128,256]{2,1,0:T(8,128)(2,1)} copy(bf16[96,128,256]{1,2,0:T(8,128)(2,1)} %fusion.1) | data formatting | bytes 12582912 | tf_op jit(solution)/shard_map/convert_element_type | solution.py:65
  38.1 4.8 %broadcast_in_dim.38 = bf16[144,128,256]{2,1,0:T(8,128)(2,1)} broadcast(bf16[]{:T(256)} %constant.33.clone.1), dimensions={} | broadcast | bytes 9437186 | tf_op jit(solution)/shard_map/broadcast_in_dim | solution.py:66
  42.9 17.7 %scatter_fusion = bf16[144,128,256]{2,1,0:T(8,128)(2,1)} fusion(bf16[144,128,256]{2,1,0:T(8,128)(2,1)} %broadcast_in_dim.38, s32[96]{0:T(128)S(1)} %fusion.32, bf16[96,128,256]{2,1,0:T(8,128)(2,1)} %copy.23), kind=kCustom, calls=%fused_computation.2 | custom fusion | bytes 18874752 | tf_op jit(solution)/shard_map/scatter | solution.py:66
  60.6 0.0 all-to-all-done
  60.6 6.3 %all-to-all-start.1 = ((bf16[16,9,128,256]{3,2,1,0:T(8,128)(2,1)}), bf16[16,9,128,256]{3,2,1,0:T(8,128)(2,1)}, u32[]{:S(2)}, u32[]{:S(2)}) async-start(bf16[16,9,128,256]{3,2,1,0:T(8,128)(2,1)} %bitcast.67), calls=%async_computation.1 | async-start | bytes 18874368 | tf_op jit(solution)/shard_map/all_to_all | solution.py:69
  66.9 11.2 %multiply_convert_fusion.3 = (bf16[1440,384]{1,0:T(8,128)(2,1)}, bf16[1440,384]{1,0:T(8,128)(2,1)}, bf16[1440,384]{1,0:T(8,128)(2,1)}, bf16[1440,384]{1,0:T(8,128)(2,1)}) fusion(s32[384]{0:T(512)S(1)} %copy-done.6, f32[384]{0:T(512)S(1)} %get-tuple-element.13, f32[384]{0:T(512)S(1)} %get-tuple-element.14), kind=kLoop, calls=%fused_computation.28 | loop fusion | flops 8847360 | bytes 4428288 | tf_op jit(solution)/shard_map/convert.12
  78.2 0.5 broadcast.173
  78.7 0.7 reduce.3
  79.4 0.1 eq.51
  79.5 156.8 %all-to-all-done.1 = bf16[16,9,128,256]{3,2,1,0:T(8,128)(2,1)} async-done(((bf16[16,9,128,256]{3,2,1,0:T(8,128)(2,1)}), bf16[16,9,128,256]{3,2,1,0:T(8,128)(2,1)}, u32[]{:S(2)}, u32[]{:S(2)}) %all-to-all-start.1) | async-done | bytes 9437216 | tf_op jit(solution)/shard_map/all_to_all | solution.py:69
  236.3 13.9 %copy.30 = bf16[18,8,128,256]{3,1,2,0:T(8,128)(2,1)} copy(bf16[18,8,128,256]{3,2,1,0:T(8,128)(2,1)} %bitcast.24) | data formatting | bytes 18874368
  250.2 5.0 %convolution_convert_fusion = bf16[45,32768]{1,0:T(8,128)(2,1)S(1)} fusion(bf16[144,32768]{1,0:T(8,128)(2,1)} %bitcast.68, s32[144]{0:T(256)S(1)} %eq.51), kind=kOutput, calls=%fused_computation.3 | convolution fusion | flops 426154304 | bytes 12386880 | tf_op jit(solution)/shard_map/dot_general | solution.py:76
  255.3 3.6 reshape.151
  258.9 5.1 %multiply_convert_fusion.1 = bf16[768,4,256]{2,0,1:T(8,128)(2,1)S(1)} fusion(bf16[4,1440,256]{2,1,0:T(8,128)(2,1)} %reshape.151, bf16[1440,384]{1,0:T(8,128)(2,1)} %get-tuple-element.12, bf16[1440,384]{1,0:T(8,128)(2,1)} %get-tuple-element.11), kind=kOutput, calls=%fused_computation.15 | convolution fusion | flops 2270920704 | bytes 6733824 | tf_op jit(solution)/shard_map/lnc,nk->lkc/dot_general | solution.py:81
  264.0 2.8 copy.25
  266.8 40.4 %all-to-all-start.2 = ((bf16[4,2,384,256]{3,1,0,2:T(2,128)(2,1)}), bf16[4,2,384,256]{3,1,0,2:T(2,128)(2,1)}, u32[]{:S(2)}, u32[]{:S(2)}) async-start(bf16[4,2,384,256]{3,1,0,2:T(2,128)(2,1)} %copy.25), calls=%async_computation.2 | async-start | bytes 3145728 | tf_op jit(solution)/shard_map/all_to_all | solution.py:85
  307.2 0.1 fusion.31
  307.3 0.2 negate_convert_fusion.1
  307.5 1.1 copy.24
  308.6 3.2 convert_element_type.101
  311.8 3.5 convert_element_type.102
  315.3 24.3 %all-to-all-done.2 = bf16[4,2,384,256]{3,1,0,2:T(2,128)(2,1)} async-done(((bf16[4,2,384,256]{3,1,0,2:T(2,128)(2,1)}), bf16[4,2,384,256]{3,1,0,2:T(2,128)(2,1)}, u32[]{:S(2)}, u32[]{:S(2)}) %all-to-all-start.2) | async-done | bytes 1572896 | tf_op jit(solution)/shard_map/all_to_all | solution.py:85
  339.6 1.7 copy.26
  341.3 0.9 copy.31
  342.2 0.6 convolution_multiply_fusion.1
  342.8 0.0 copy-start.2
  342.8 1.0 copy.32
  343.8 0.9 copy-done.2
  344.7 0.5 subtract_convert_fusion
  345.1 0.1 pad_maximum_fusion
  345.3 0.4 copy.33
  345.7 0.6 fusion
  346.3 0.4 copy.34
  346.7 45.1 %all_to_all.44 = bf16[64,2,24,256]{3,2,1,0:T(8,128)(2,1)S(1)} all-to-all(bf16[64,2,24,256]{3,2,1,0:T(8,128)(2,1)S(1)} %bitcast.75), channel_id=1, replica_groups=mesh['grp'=2,'band'=16] {'band'}, dimensions={0} | all-to-all | bytes 3145728 | tf_op jit(solution)/shard_map/all_to_all | solution.py:105
  391.8 0.1 copy.28
  392.0 1.7 copy-done.3
  393.7 4.2 %fusion.5 = bf16[4,1440,256]{2,1,0:T(8,128)(2,1)} fusion(bf16[4,1440,256]{2,1,0:T(8,128)(2,1)S(1)} %copy-done.3, bf16[4,768,256]{2,1,0:T(8,128)(2,1)S(1)} %bitcast.78, bf16[1440,384]{1,0:T(8,128)(2,1)S(1)} %copy-done.5, bf16[1440,384]{1,0:T(8,128)(2,1)S(1)} %copy-done.4), kind=kOutput, calls=%fused_computation.13 | convolution fusion | flops 2275246080 | bytes 9682944 | tf_op jit(solution)/shard_map/lkc,kn->lnc/dot_general | solution.py:106
  (15 shorter events, 0.1 us)
Async XLA Ops:
  0.0 21.1 %copy-start = (bf16[96,128,128]{2,1,0:T(8,128)(2,1)S(1)}, bf16[96,128,128]{2,1,0:T(8,128)(2,1)}, u32[]{:S(2)}) copy-start(bf16[96,128,128]{2,1,0:T(8,128)(2,1)} %param.9) | copy-start | bytes 9437188
  4.2 56.4 %all-to-all-start = ((s32[16,1,9]{2,1,0:T(1,128)}), s32[16,1,9]{2,1,0:T(1,128)S(1)}, u32[]{:S(2)}, u32[]{:S(2)}) async-start(s32[16,1,9]{2,1,0:T(1,128)} %bitcast.3), calls=%async_computation | async-start | bytes 16384 | tf_op jit(solution)/shard_map/all_to_all | solution.py:70
  60.6 6.3 %copy-start.6 = (s32[384]{0:T(512)S(1)}, s32[384]{0:T(512)}, u32[]{:S(2)}) copy-start(s32[384]{0:T(512)} %param.14) | copy-start | bytes 4612
  60.6 175.7 %all-to-all-start.1 = ((bf16[16,9,128,256]{3,2,1,0:T(8,128)(2,1)}), bf16[16,9,128,256]{3,2,1,0:T(8,128)(2,1)}, u32[]{:S(2)}, u32[]{:S(2)}) async-start(bf16[16,9,128,256]{3,2,1,0:T(8,128)(2,1)} %bitcast.67), calls=%async_computation.1 | async-start | bytes 18874368 | tf_op jit(solution)/shard_map/all_to_all | solution.py:69
  266.8 72.8 %all-to-all-start.2 = ((bf16[4,2,384,256]{3,1,0,2:T(2,128)(2,1)}), bf16[4,2,384,256]{3,1,0,2:T(2,128)(2,1)}, u32[]{:S(2)}, u32[]{:S(2)}) async-start(bf16[4,2,384,256]{3,1,0,2:T(2,128)(2,1)} %copy.25), calls=%async_computation.2 | async-start | bytes 3145728 | tf_op jit(solution)/shard_map/all_to_all | solution.py:85
  342.8 1.9 copy-start.2
  346.7 45.3 %copy-start.4 = (bf16[1440,384]{1,0:T(8,128)(2,1)S(1)}, bf16[1440,384]{1,0:T(8,128)(2,1)}, u32[]{:S(2)}) copy-start(bf16[1440,384]{1,0:T(8,128)(2,1)} %get-tuple-element.9) | copy-start | bytes 3317764
  346.7 45.3 %copy-start.5 = (bf16[1440,384]{1,0:T(8,128)(2,1)S(1)}, bf16[1440,384]{1,0:T(8,128)(2,1)}, u32[]{:S(2)}) copy-start(bf16[1440,384]{1,0:T(8,128)(2,1)} %get-tuple-element.10) | copy-start | bytes 3317764
  391.8 1.8 copy-start.3
  393.7 4.2 %copy-start.1 = (bf16[96,128,128]{2,1,0:T(8,128)(2,1)S(1)}, bf16[96,128,128]{2,1,0:T(8,128)(2,1)}, u32[]{:S(2)}) copy-start(bf16[96,128,128]{2,1,0:T(8,128)(2,1)} %param.9) | copy-start | bytes 9437188
where the time goes:
time: 399 us; the launch traced here: 398 us
  waiting for transfers between devices  181 us (45%)
  local copies, waits for them, and re-layouts  72.7 us (18%)
  starting transfers between devices  54 us (14%)
  blocking collectives  45.1 us (11%)
  matrix products  23.9 us (6%)
  other arithmetic  20.2 us (5%)
    all_to_all x1, waiting for transfers between devices, per_device(): lax.all_to_all(sending, 'band', split_axis=0, concat_axis=0, tiled=True)  157 us
    all_to_all x1, blocking collectives, per_device(): lax.all_to_all(back, 'band', split_axis=0, concat_axis=2, tiled=True)  45.1 us
    all_to_all x1, starting transfers between devices, per_device(): lax.all_to_all(spectrum, 'band', split_axis=2, concat_axis=0, tiled=True)  40.4 us
    all_to_all x1, waiting for transfers between devices, per_device(): lax.all_to_all(spectrum, 'band', split_axis=2, concat_axis=0, tiled=True)  24.3 us
    unnamed x19, local copies, waits for them, and re-layouts  19.2 us
    scatter x1, local copies, waits for them, and re-layouts, per_device(): jnp.zeros((total_slots, pixels, channels), jnp.bfloat16).at[position]  17.7 us
    another operation x4, other arithmetic  12 us
    convert_element_type x1, local copies, waits for them, and re-layouts, per_device(): (made * valid.astype(jnp.float32)[:, None, None]).astype(jnp.bfloat16)  8.62 us
  transfers between devices with their start and end apart: 3, of which 2 were waited for; matrix products, arithmetic and copies ran while one was open for 17% of the time, Pallas kernels for 0%

commit v1 on v0

v1 whole, which is shorter than its diff:
```python
import math

import jax
import jax.numpy as jnp
from jax import lax
from jax.experimental import pallas as pl
from jax.experimental.pallas import tpu as pltpu
from jax.sharding import PartitionSpec as P

NLON = 1440
LAT_DEV = 4
TB_DEV = 45
CHUNKS = 2


def lon_tables(mode_index, bands):
    grid_n = jnp.arange(NLON, dtype=jnp.int32)
    phase = grid_n[:, None] * mode_index[None, :] % NLON
    angle = phase.astype(jnp.float32) * (2.0 * math.pi / NLON)
    modes = mode_index.shape[0]
    factor = jnp.where((mode_index == 0) | (mode_index == NLON // 2), 1.0, 2.0).astype(jnp.float32)
    cosine = jnp.cos(angle)
    sine = jnp.sin(angle)

    def by_owner(a, b):
        both = [a.reshape(NLON, bands, 1, -1), b.reshape(NLON, bands, 1, -1)]
        return jnp.concatenate(both, axis=2).reshape(NLON, 2 * modes).astype(jnp.bfloat16)

    forward = by_owner(cosine, -sine)
    inverse = by_owner(factor[None, :] * cosine, -factor[None, :] * sine)
    return forward, inverse


def lat_table(nlat):
    index = jnp.arange(nlat, dtype=jnp.int32)
    phase = index[:, None] * index[None, :] % nlat
    angle = phase.astype(jnp.float32) * (2.0 * math.pi / nlat)
    cosine = jnp.cos(angle)
    sine = jnp.sin(angle)
    upper = jnp.stack([cosine, sine], axis=2)
    lower = jnp.stack([-sine, cosine], axis=2)
    table = jnp.stack([upper, lower], axis=1)
    return table.reshape(2 * nlat, 2 * nlat).astype(jnp.bfloat16)


def make_kernel(slots, entry_ref, source_ref, weight_ref, field_ref, out_ref):
    band = pl.program_id(0)
    for slot in range(slots):
        at = band * slots + slot
        out_ref[0, slot] = jnp.dot(
            weight_ref[entry_ref[at]],
            field_ref[source_ref[at]],
            preferred_element_type=jnp.float32,
        ).astype(out_ref.dtype)


def make_contributions(entry, source, weight, field, bands, slots, part, width):
    pixels = field.shape[1]
    return pl.pallas_call(
        lambda *refs: make_kernel(slots, *refs),
        out_shape=jax.ShapeDtypeStruct((bands, slots, pixels, width), jnp.bfloat16),
        grid_spec=pltpu.PrefetchScalarGridSpec(
            num_scalar_prefetch=2,
            grid=(bands,),
            in_specs=[
                pl.BlockSpec(weight.shape, lambda b, *_: (0, 0, 0)),
                pl.BlockSpec((field.shape[0], pixels, width), lambda b, *_: (0, 0, part)),
            ],
            out_specs=pl.BlockSpec((1, slots, pixels, width), lambda b, *_: (b, 0, 0, 0)),
        ),
        compiler_params=pltpu.CompilerParams(vmem_limit_bytes=32 * 2**20),
        cost_estimate=pl.CostEstimate(
            flops=2 * bands * slots * pixels * pixels * width * 4,
            bytes_accessed=2 * bands * slots * pixels * width,
            transcendentals=0,
        ),
        name="make_contributions",
    )(entry, source, weight, field)


def regrid_kernel(bands, slots, ids_ref, arrived_ref, out_ref, total_ref):
    band = pl.program_id(0)

    @pl.when(band == 0)
    def _():
        total_ref[...] = jnp.zeros_like(total_ref)

    for slot in range(slots):
        block = ids_ref[band * slots + slot]

        @pl.when(block >= 0)
        def _():
            total_ref[block] += arrived_ref[0, slot].astype(jnp.float32)

    @pl.when(band == bands - 1)
    def _():
        out_ref[...] = total_ref[...].astype(out_ref.dtype)


def regrid(ids, arrived):
    bands, slots, pixels, width = arrived.shape
    return pl.pallas_call(
        lambda *refs: regrid_kernel(bands, slots, *refs),
        out_shape=jax.ShapeDtypeStruct((TB_DEV, pixels, width), jnp.bfloat16),
        grid_spec=pltpu.PrefetchScalarGridSpec(
            num_scalar_prefetch=1,
            grid=(bands,),
            in_specs=[pl.BlockSpec((1, slots, pixels, width), lambda b, *_: (b, 0, 0, 0))],
            out_specs=pl.BlockSpec((TB_DEV, pixels, width), lambda b, *_: (0, 0, 0)),
            scratch_shapes=[pltpu.VMEM((TB_DEV, pixels, width), jnp.float32)],
        ),
        compiler_params=pltpu.CompilerParams(vmem_limit_bytes=32 * 2**20),
        cost_estimate=pl.CostEstimate(
            flops=bands * slots * pixels * width,
            bytes_accessed=2 * bands * slots * pixels * width + 2 * TB_DEV * pixels * width,
            transcendentals=0,
        ),
        name="regrid",
    )(ids, arrived)


def per_device(
    source_field,
    interp_weight,
    dest_band,
    target_block,
    source_block,
    entry_count,
    mode_index,
    filter_weight,
):
    bands = lax.axis_size("band")
    entries = interp_weight.shape[0]
    slots = max(2, 3 * entries // (2 * bands))
    total_slots = bands * slots
    channels = source_field.shape[2]
    width = channels // CHUNKS
    modes = mode_index.shape[0]
    mode_dev = modes // bands
    nlat = LAT_DEV * bands

    entry_ids = jnp.arange(entries, dtype=jnp.int32)
    dest = dest_band[:, 0]
    valid = entry_ids < entry_count[0]

    earlier = (dest[:, None] == dest[None, :]) & (entry_ids[:, None] > entry_ids[None, :])
    rank = jnp.sum(earlier.astype(jnp.int32), axis=1)
    position = dest * slots + rank
    slot_ids = jnp.arange(total_slots, dtype=jnp.int32)
    placed = slot_ids[:, None] == position[None, :]
    entry_of = jnp.sum(jnp.where(placed, entry_ids[None, :], 0), axis=1)
    source_of = jnp.sum(jnp.where(placed, source_block[None, :], 0), axis=1)
    target_of = jnp.max(
        jnp.where(placed & valid[None, :], target_block[None, :], -1), axis=1
    ).reshape(bands, slots)

    ids = lax.all_to_all(target_of, "band", split_axis=0, concat_axis=0, tiled=True)
    ids = ids.reshape(total_slots)

    sent = []
    for part in range(CHUNKS):
        made = make_contributions(
            entry_of, source_of, interp_weight, source_field, bands, slots, part, width
        )
        sent.append(lax.all_to_all(made, "band", split_axis=0, concat_axis=0, tiled=True))

    forward, inverse = lon_tables(mode_index, bands)
    table = lat_table(nlat)
    filt = filter_weight.astype(jnp.float32)
    grids, returned = [], []
    for part in range(CHUNKS):
        grid = regrid(ids, sent[part]).reshape(LAT_DEV, NLON, width)
        grids.append(grid)
        spectrum = jnp.einsum(
            "lnc,nk->lkc", grid, forward, preferred_element_type=jnp.float32
        ) * (1.0 / math.sqrt(NLON))
        spectrum = spectrum.astype(jnp.bfloat16).reshape(LAT_DEV, bands, 2 * mode_dev, width)
        spectrum = spectrum.transpose(1, 0, 2, 3)
        pencils = lax.all_to_all(spectrum, "band", split_axis=0, concat_axis=0, tiled=True)
        mixed = jnp.dot(
            table,
            pencils.reshape(2 * nlat, mode_dev * width),
            preferred_element_type=jnp.float32,
        ) * (1.0 / math.sqrt(nlat))
        mixed = mixed.reshape(nlat, 2, mode_dev, width)
        own = filt[..., part * width : (part + 1) * width]
        real_part = own[:, 0] * mixed[:, 0] - own[:, 1] * mixed[:, 1]
        imag_part = own[:, 0] * mixed[:, 1] + own[:, 1] * mixed[:, 0]
        shaped = (
            jnp.stack([real_part, imag_part], axis=1)
            .astype(jnp.bfloat16)
            .reshape(2 * nlat, mode_dev * width)
        )
        back = lax.dot_general(
            table, shaped, (((0,), (0,)), ((), ())), preferred_element_type=jnp.float32
        ) * (1.0 / math.sqrt(nlat))
        back = back.astype(jnp.bfloat16).reshape(bands, LAT_DEV, 2 * mode_dev, width)
        back = lax.all_to_all(back, "band", split_axis=0, concat_axis=0, tiled=True)
        returned.append(back.transpose(1, 0, 2, 3).reshape(LAT_DEV, 2 * modes, width))

    filtered = jnp.einsum(
        "lkc,nk->lnc",
        jnp.concatenate(returned, axis=2),
        inverse,
        preferred_element_type=jnp.float32,
    ) * (1.0 / math.sqrt(NLON))
    regridded = jnp.concatenate(grids, axis=2)
    processed = (regridded.astype(jnp.float32) + filtered).astype(jnp.bfloat16)
    return processed.reshape(LAT_DEV * NLON, channels)


def solution(mesh):
    in_specs = (
        P(("grp", "band"), None, None),
        P("band", None, None),
        P("band", None),
        P("band"),
        P("band"),
        P("band"),
        P(),
        P(None, None, "band", None),
    )
    out_specs = P(("grp", "band"), None)
    return jax.shard_map(
        per_device, mesh=mesh, in_specs=in_specs, out_specs=out_specs, check_vma=False
    )
```

time: 399 us -> 355 us (0.89)
  blocking collectives: 45.1 us -> 0 us
  local copies, waits for them, and re-layouts: 72.7 us -> 33.4 us
  Pallas kernels: 0 us -> 29 us
  starting transfers between devices: 54 us -> 73.3 us
  matrix products: 23.9 us -> 14.5 us
  other arithmetic: 20.2 us -> 26.2 us
  waiting for transfers between devices: 181 us -> 176 us
    all_to_all x1 -> x0, blocking collectives: 45.1 us -> none  [per_device(): lax.all_to_all(back, 'band', split_axis=0, concat_axis=2, tiled=True)]
    pallas_call x0 -> x4, Pallas kernels: none -> 29 us  [the longest x2 19.6 us: regrid(): pl.pallas_call(lambda *refs: regrid_kernel(bands, slots, *refs), out_shap...]
    all_to_all x3 -> x7, starting transfers between devices: 54 us -> 73.3 us  [the longest x2 27.7 us: per_device(): lax.all_to_all(made, 'band', split_axis=0, concat_axis=0, tiled=True)]
    scatter x2 -> x0, local copies, waits for them, and re-layouts: 18.7 us -> none  [the longest x1 17.7 us: per_device(): jnp.zeros((total_slots, pixels, channels), jnp.bfloat16).at[position]]
    dot_general x5, matrix products: 23.3 us -> 11.9 us  [the longest x1 6.04 us: per_device(): jnp.einsum('lkc,nk->lnc', jnp.concatenate(returned, axis=2), inverse, pre...]
    convert_element_type x1 -> x0, local copies, waits for them, and re-layouts: 8.62 us -> none  [per_device(): (made * valid.astype(jnp.float32)[:, None, None]).astype(jnp.bfloat16)]
    gather x1 -> x0, local copies, waits for them, and re-layouts: 7.57 us -> none  [per_device(): picked = jnp.take(source_field, source_block, axis=0)]
    unnamed x19 -> x24, local copies, waits for them, and re-layouts: 19.2 us -> 11.7 us
  transfers between devices with their start and end apart: 3 -> 7, of which waited for: 2 -> 6; matrix products, arithmetic and copies ran while one was open for 17% -> 13% of each run, Pallas kernels for 0% -> 8%
where the time goes in v1:
time: 355 us; the launch traced here: 353 us
  waiting for transfers between devices  176 us (50%)
  starting transfers between devices  73.3 us (21%)
  local copies, waits for them, and re-layouts  33.4 us (9%)
  Pallas kernels  29 us (8%)
  other arithmetic  26.2 us (7%)
  matrix products  14.5 us (4%)
    all_to_all x2, waiting for transfers between devices, per_device(): lax.all_to_all(made, 'band', split_axis=0, concat_axis=0, tiled=True)  138 us
    all_to_all x2, starting transfers between devices, per_device(): lax.all_to_all(made, 'band', split_axis=0, concat_axis=0, tiled=True)  27.7 us
    all_to_all x2, waiting for transfers between devices, per_device(): back = lax.all_to_all(back, 'band', split_axis=0, concat_axis=0, tiled=True)  27.4 us
    all_to_all x2, starting transfers between devices, per_device(): lax.all_to_all(spectrum, 'band', split_axis=0, concat_axis=0, tiled=True)  27 us
    pallas_call x2, Pallas kernels, regrid(): pl.pallas_call(lambda *refs: regrid_kernel(bands, slots, *refs), out_shap...  19.6 us
    another operation x4, other arithmetic  13.4 us
    unnamed x24, local copies, waits for them, and re-layouts  11.7 us
    all_to_all x2, starting transfers between devices, per_device(): back = lax.all_to_all(back, 'band', split_axis=0, concat_axis=0, tiled=True)  11.3 us
  transfers between devices with their start and end apart: 7, of which 6 were waited for; matrix products, arithmetic and copies ran while one was open for 13% of the time, Pallas kernels for 8%

profile of v1, /device:TPU:1, one launch (start us, length us, event | category | flops | bytes accessed | tf_op | source)
XLA Modules:
  0.0 353.2 jit_solution(12567648349728739047)
XLA Ops:
  0.0 0.9 convert_reduce_fusion
  2.2 0.9 select_reduce_fusion
  3.8 7.3 %all-to-all-start = ((s32[16,1,9]{2,1,0:T(1,128)}), s32[16,1,9]{2,1,0:T(1,128)S(1)}, u32[]{:S(2)}, u32[]{:S(2)}) async-start(s32[16,1,9]{2,1,0:T(1,128)} %bitcast.2), calls=%async_computation | async-start | bytes 16384 | tf_op jit(solution)/shard_map/all_to_all | solution.py:157
  11.2 1.9 copy-done.2
  13.0 1.6 copy-done.4
  14.6 4.7 %make_contributions.2 = bf16[16,9,128,128]{3,2,1,0:T(8,128)(2,1)S(1)} custom-call(s32[144]{0:T(256)S(1)} %get-tuple-element.6.refs_0_, s32[144]{0:T(256)S(1)} %get-tuple-element.5.refs_1_, bf16[96,128,128]{2,1,0:T(8,128)(2,1)S(1)} %copy-done.2, bf16[32,128,256]{2,1,0:T(8,128)(2,1)S(1)} %copy-done.4), custom_call_target="tpu_custom_call" | custom-call | flops 2415919104 | bytes 4718592 | tf_op jit(solution)/shard_map/make_contributions/pallas_call | solution.py:59
  19.3 2.1 copy-done.1
  21.5 6.3 %all-to-all-start.1 = ((bf16[16,9,128,128]{3,2,1,0:T(8,128)(2,1)}), bf16[16,9,128,128]{3,2,1,0:T(8,128)(2,1)}, u32[]{:S(2)}, u32[]{:S(2)}) async-start(bf16[16,9,128,128]{3,2,1,0:T(8,128)(2,1)} %copy-done.1), calls=%async_computation.1 | async-start | bytes 9437184 | tf_op jit(solution)/shard_map/all_to_all | solution.py:165
  27.8 1.6 copy-done.5
  29.4 4.7 %make_contributions.3 = bf16[16,9,128,128]{3,2,1,0:T(8,128)(2,1)S(1)} custom-call(s32[144]{0:T(256)S(1)} %get-tuple-element.6.refs_0_, s32[144]{0:T(256)S(1)} %get-tuple-element.5.refs_1_, bf16[96,128,128]{2,1,0:T(8,128)(2,1)S(1)} %copy-done.3, bf16[32,128,256]{2,1,0:T(8,128)(2,1)S(1)} %copy-done.5), custom_call_target="tpu_custom_call" | custom-call | flops 2415919104 | bytes 4718592 | tf_op jit(solution)/shard_map/make_contributions/pallas_call | solution.py:59
  34.1 2.2 copy-done
  36.2 78.7 %all-to-all-done.1.refs_1_ = bf16[16,9,128,128]{3,2,1,0:T(8,128)(2,1)} async-done(((bf16[16,9,128,128]{3,2,1,0:T(8,128)(2,1)}), bf16[16,9,128,128]{3,2,1,0:T(8,128)(2,1)}, u32[]{:S(2)}, u32[]{:S(2)}) %all-to-all-start.1) | async-done | bytes 4718624 | tf_op jit(solution)/shard_map/all_to_all | solution.py:165
  115.0 21.4 %all-to-all-start.2 = ((bf16[16,9,128,128]{3,2,1,0:T(8,128)(2,1)}), bf16[16,9,128,128]{3,2,1,0:T(8,128)(2,1)}, u32[]{:S(2)}, u32[]{:S(2)}) async-start(bf16[16,9,128,128]{3,2,1,0:T(8,128)(2,1)} %copy-done), calls=%async_computation.2 | async-start | bytes 9437184 | tf_op jit(solution)/shard_map/all_to_all | solution.py:165
  136.7 12.0 %fusion.9 = (bf16[1440,16,1,24]{0,3,2,1:T(8,128)(2,1)S(1)}, bf16[1440,16,1,24]{0,3,2,1:T(8,128)(2,1)S(1)}, bf16[1440,16,1,24]{0,3,2,1:T(8,128)(2,1)}, bf16[1440,16,1,24]{0,3,2,1:T(8,128)(2,1)}) fusion(s32[16,24]{1,0:T(8,128)S(1)} %mul.242, f32[16,24]{1,0:T(8,128)S(1)} %mul.248, f32[16,24]{1,0:T(8,128)S(1)} %mul.239), kind=kLoop, calls=%fused_computation.21 | loop fusion | flops 8847360 | bytes 4428288 | tf_op jit(solution)/shard_map/convert.4
  148.6 1.6 pad_maximum_fusion.1
  151.7 9.8 %regrid.2 = bf16[45,128,128]{2,1,0:T(8,128)(2,1)S(1)} custom-call(s32[144]{0:T(256)S(1)} %reshape.296.refs_0_, bf16[16,9,128,128]{3,2,1,0:T(8,128)(2,1)} %all-to-all-done.1.refs_1_), custom_call_target="tpu_custom_call" | custom-call | flops 2359296 | bytes 6193152 | tf_op jit(solution)/shard_map/regrid/pallas_call | solution.py:102
  161.5 1.4 multiply_convert_fusion.3
  162.9 1.0 copy.58
  163.9 59.7 %all-to-all-done.2.refs_1_ = bf16[16,9,128,128]{3,2,1,0:T(8,128)(2,1)} async-done(((bf16[16,9,128,128]{3,2,1,0:T(8,128)(2,1)}), bf16[16,9,128,128]{3,2,1,0:T(8,128)(2,1)}, u32[]{:S(2)}, u32[]{:S(2)}) %all-to-all-start.2) | async-done | bytes 4718624 | tf_op jit(solution)/shard_map/all_to_all | solution.py:165
  223.6 21.4 %all-to-all-start.3 = ((bf16[16,4,48,128]{3,2,1,0:T(8,128)(2,1)}), bf16[16,4,48,128]{3,2,1,0:T(8,128)(2,1)}, u32[]{:S(2)}, u32[]{:S(2)}) async-start(bf16[16,4,48,128]{3,2,1,0:T(8,128)(2,1)} %bitcast.72), calls=%async_computation.3 | async-start | bytes 1572864 | tf_op jit(solution)/shard_map/all_to_all | solution.py:179
  245.0 9.8 %regrid.3 = bf16[45,128,128]{2,1,0:T(8,128)(2,1)S(1)} custom-call(s32[144]{0:T(256)S(1)} %reshape.296.refs_0_, bf16[16,9,128,128]{3,2,1,0:T(8,128)(2,1)} %all-to-all-done.2.refs_1_), custom_call_target="tpu_custom_call" | custom-call | flops 2359296 | bytes 6193152 | tf_op jit(solution)/shard_map/regrid/pallas_call | solution.py:102
  254.8 1.4 multiply_convert_fusion.2
  256.2 1.0 copy.57
  257.2 6.5 %all-to-all-done.3 = bf16[16,4,48,128]{3,2,1,0:T(8,128)(2,1)} async-done(((bf16[16,4,48,128]{3,2,1,0:T(8,128)(2,1)}), bf16[16,4,48,128]{3,2,1,0:T(8,128)(2,1)}, u32[]{:S(2)}, u32[]{:S(2)}) %all-to-all-start.3) | async-done | bytes 786464 | tf_op jit(solution)/shard_map/all_to_all | solution.py:179
  263.6 5.6 %all-to-all-start.5 = ((bf16[16,4,48,128]{3,2,1,0:T(8,128)(2,1)}), bf16[16,4,48,128]{3,2,1,0:T(8,128)(2,1)}, u32[]{:S(2)}, u32[]{:S(2)}) async-start(bf16[16,4,48,128]{3,2,1,0:T(8,128)(2,1)} %bitcast.80), calls=%async_computation.5 | async-start | bytes 1572864 | tf_op jit(solution)/shard_map/all_to_all | solution.py:179
  269.6 2.0 copy.29
  271.6 4.2 %convert_element_type.143 = bf16[128,128]{1,0:T(8,128)(2,1)S(1)} reshape(bf16[64,2,64,2]{3,2,1,0:T(8,128)(2,1)} %copy.29) | data formatting | bytes 65536 | tf_op jit(solution)/shard_map/convert_element_type | solution.py:43
  275.8 3.5 convert_element_type.144
  279.3 2.2 reshape.300
  281.4 1.5 fusion.14
  282.9 1.4 copy.43
  284.3 3.6 %all-to-all-done.5 = bf16[16,4,48,128]{3,2,1,0:T(8,128)(2,1)} async-done(((bf16[16,4,48,128]{3,2,1,0:T(8,128)(2,1)}), bf16[16,4,48,128]{3,2,1,0:T(8,128)(2,1)}, u32[]{:S(2)}, u32[]{:S(2)}) %all-to-all-start.5) | async-done | bytes 786464 | tf_op jit(solution)/shard_map/all_to_all | solution.py:179
  287.9 2.2 reshape.305
  290.1 1.6 fusion.15
  292.7 1.2 subtract_convert_fusion.1
  293.9 1.3 fusion.2
  295.2 2.2 reshape.307
  297.4 5.6 %all-to-all-start.6 = ((bf16[16,4,48,128]{3,2,1,0:T(8,128)(2,1)}), bf16[16,4,48,128]{3,2,1,0:T(8,128)(2,1)}, u32[]{:S(2)}, u32[]{:S(2)}) async-start(bf16[16,4,48,128]{3,2,1,0:T(8,128)(2,1)} %reshape.307), calls=%async_computation.6 | async-start | bytes 1572864 | tf_op jit(solution)/shard_map/all_to_all | solution.py:198
  303.1 1.1 pad_maximum_fusion.2
  304.1 1.3 fusion.1
  305.4 2.2 reshape.302
  307.6 14.1 %all-to-all-done.6 = bf16[16,4,48,128]{3,2,1,0:T(8,128)(2,1)} async-done(((bf16[16,4,48,128]{3,2,1,0:T(8,128)(2,1)}), bf16[16,4,48,128]{3,2,1,0:T(8,128)(2,1)}, u32[]{:S(2)}, u32[]{:S(2)}) %all-to-all-start.6) | async-done | bytes 786464 | tf_op jit(solution)/shard_map/all_to_all | solution.py:198
  321.7 5.6 %all-to-all-start.4 = ((bf16[16,4,48,128]{3,2,1,0:T(8,128)(2,1)}), bf16[16,4,48,128]{3,2,1,0:T(8,128)(2,1)}, u32[]{:S(2)}, u32[]{:S(2)}) async-start(bf16[16,4,48,128]{3,2,1,0:T(8,128)(2,1)} %reshape.302), calls=%async_computation.4 | async-start | bytes 1572864 | tf_op jit(solution)/shard_map/all_to_all | solution.py:198
  327.4 3.3 pad_maximum_fusion
  330.6 2.1 copy.35
  332.7 13.3 %all-to-all-done.4 = bf16[16,4,48,128]{3,2,1,0:T(8,128)(2,1)} async-done(((bf16[16,4,48,128]{3,2,1,0:T(8,128)(2,1)}), bf16[16,4,48,128]{3,2,1,0:T(8,128)(2,1)}, u32[]{:S(2)}, u32[]{:S(2)}) %all-to-all-start.4) | async-done | bytes 786464 | tf_op jit(solution)/shard_map/all_to_all | solution.py:198
  346.0 1.2 copy.32
  347.2 6.0 %fusion = bf16[4,1440,256]{2,1,0:T(8,128)(2,1)} fusion(bf16[1440,768,1]{0,1,2:T(8,128)(2,1)} %bitcast.85, bf16[4,1440,128]{2,1,0:T(8,128)(2,1)S(1)} %bitcast.77, bf16[4,1440,128]{2,1,0:T(8,128)(2,1)S(1)} %bitcast.75, bf16[4,768,128]{2,1,0:T(8,128)(2,1)} %bitcast.86, bf16[4,768,128]{2,1,0:T(8,128)(2,1)S(1)} %bitcast.87), kind=kOutput, calls=%fused_computation.1 | convolution fusion | flops 2278391808 | bytes 9682944 | tf_op jit(solution)/shard_map/lkc,nk->lnc/dot_general | solution.py:201
  (34 shorter events, 4.4 us)
Async XLA Ops:
  3.8 17.7 %all-to-all-start = ((s32[16,1,9]{2,1,0:T(1,128)}), s32[16,1,9]{2,1,0:T(1,128)S(1)}, u32[]{:S(2)}, u32[]{:S(2)}) async-start(s32[16,1,9]{2,1,0:T(1,128)} %bitcast.2), calls=%async_computation | async-start | bytes 16384 | tf_op jit(solution)/shard_map/all_to_all | solution.py:157
  11.1 1.9 copy-start.2
  13.0 1.6 copy-start.4
  19.3 2.1 copy-start.1
  21.5 6.3 %copy-start.3 = (bf16[96,128,128]{2,1,0:T(8,128)(2,1)S(1)}, bf16[96,128,128]{2,1,0:T(8,128)(2,1)}, u32[]{:S(2)}) copy-start(bf16[96,128,128]{2,1,0:T(8,128)(2,1)} %refs_2_.3) | copy-start | bytes 9437188
  21.5 93.5 %all-to-all-start.1 = ((bf16[16,9,128,128]{3,2,1,0:T(8,128)(2,1)}), bf16[16,9,128,128]{3,2,1,0:T(8,128)(2,1)}, u32[]{:S(2)}, u32[]{:S(2)}) async-start(bf16[16,9,128,128]{3,2,1,0:T(8,128)(2,1)} %copy-done.1), calls=%async_computation.1 | async-start | bytes 9437184 | tf_op jit(solution)/shard_map/all_to_all | solution.py:165
  27.8 1.6 copy-start.5
  34.1 2.2 copy-start
  36.2 100.1 %copy-start.10 = (s32[384]{0:T(512)S(1)}, s32[384]{0:T(512)}, u32[]{:S(2)}) copy-start(s32[384]{0:T(512)} %param.14) | copy-start | bytes 4612
  115.0 108.6 %all-to-all-start.2 = ((bf16[16,9,128,128]{3,2,1,0:T(8,128)(2,1)}), bf16[16,9,128,128]{3,2,1,0:T(8,128)(2,1)}, u32[]{:S(2)}, u32[]{:S(2)}) async-start(bf16[16,9,128,128]{3,2,1,0:T(8,128)(2,1)} %copy-done), calls=%async_computation.2 | async-start | bytes 9437184 | tf_op jit(solution)/shard_map/all_to_all | solution.py:165
  151.6 9.8 %copy-start.8 = (bf16[1440,16,2,24]{0,3,2,1:T(8,128)(2,1)S(1)}, bf16[1440,16,2,24]{0,3,2,1:T(8,128)(2,1)}, u32[]{:S(2)}) copy-start(bf16[1440,16,2,24]{0,3,2,1:T(8,128)(2,1)} %pad_maximum_fusion.1) | copy-start | bytes 6635524
  223.6 40.1 %all-to-all-start.3 = ((bf16[16,4,48,128]{3,2,1,0:T(8,128)(2,1)}), bf16[16,4,48,128]{3,2,1,0:T(8,128)(2,1)}, u32[]{:S(2)}, u32[]{:S(2)}) async-start(bf16[16,4,48,128]{3,2,1,0:T(8,128)(2,1)} %bitcast.72), calls=%async_computation.3 | async-start | bytes 1572864 | tf_op jit(solution)/shard_map/all_to_all | solution.py:179
  245.0 9.8 %copy-start.9 = (bf16[1440,16,2,24]{0,3,2,1:T(8,128)(2,1)S(1)}, bf16[1440,16,2,24]{0,3,2,1:T(8,128)(2,1)}, u32[]{:S(2)}) copy-start(bf16[1440,16,2,24]{0,3,2,1:T(8,128)(2,1)} %pad_maximum_fusion.1) | copy-start | bytes 6635524
  263.6 24.3 %all-to-all-start.5 = ((bf16[16,4,48,128]{3,2,1,0:T(8,128)(2,1)}), bf16[16,4,48,128]{3,2,1,0:T(8,128)(2,1)}, u32[]{:S(2)}, u32[]{:S(2)}) async-start(bf16[16,4,48,128]{3,2,1,0:T(8,128)(2,1)} %bitcast.80), calls=%async_computation.5 | async-start | bytes 1572864 | tf_op jit(solution)/shard_map/all_to_all | solution.py:179
  290.1 2.1 copy-start.6
  290.1 2.6 copy-start.7
  297.4 24.3 %all-to-all-start.6 = ((bf16[16,4,48,128]{3,2,1,0:T(8,128)(2,1)}), bf16[16,4,48,128]{3,2,1,0:T(8,128)(2,1)}, u32[]{:S(2)}, u32[]{:S(2)}) async-start(bf16[16,4,48,128]{3,2,1,0:T(8,128)(2,1)} %reshape.307), calls=%async_computation.6 | async-start | bytes 1572864 | tf_op jit(solution)/shard_map/all_to_all | solution.py:198
  321.7 24.3 %all-to-all-start.4 = ((bf16[16,4,48,128]{3,2,1,0:T(8,128)(2,1)}), bf16[16,4,48,128]{3,2,1,0:T(8,128)(2,1)}, u32[]{:S(2)}, u32[]{:S(2)}) async-start(bf16[16,4,48,128]{3,2,1,0:T(8,128)(2,1)} %reshape.302), calls=%async_computation.4 | async-start | bytes 1572864 | tf_op jit(solution)/shard_map/all_to_all | solution.py:198

commit v2 on v0

v2 whole, which is shorter than its diff:
```python
import math

import jax
import jax.numpy as jnp
from jax import lax
from jax.experimental import pallas as pl
from jax.experimental.pallas import tpu as pltpu
from jax.sharding import PartitionSpec as P

NLON = 1440
LAT_DEV = 4
TB_DEV = 45
CHUNKS = 2


def lon_table(mode_index, bands, rows):
    step = 36
    high = jnp.arange(0, NLON, step, dtype=jnp.int32)
    low = jnp.arange(step, dtype=jnp.int32)

    def waves(index):
        phase = mode_index[:, None] * index[None, :] % NLON
        angle = phase.astype(jnp.float32) * (2.0 * math.pi / NLON)
        return jnp.cos(angle), jnp.sin(angle)

    cos_high, sin_high = [w[:, :, None] for w in waves(high)]
    cos_low, sin_low = [w[:, None, :] for w in waves(low)]
    modes = mode_index.shape[0]
    cosine = (cos_high * cos_low - sin_high * sin_low).reshape(bands, 1, modes // bands, NLON)
    sine = (sin_high * cos_low + cos_high * sin_low).reshape(bands, 1, modes // bands, NLON)
    forward = jnp.concatenate([cosine, -sine], axis=1).astype(jnp.bfloat16)
    forward = forward.reshape(bands, 2 * (modes // bands), NLON)
    forward = jnp.pad(forward, ((0, 0), (0, rows - forward.shape[1]), (0, 0)))
    return forward.reshape(bands * rows, NLON)


def lat_table(nlat):
    index = jnp.arange(nlat, dtype=jnp.int32)
    phase = index[:, None] * index[None, :] % nlat
    angle = phase.astype(jnp.float32) * (2.0 * math.pi / nlat)
    cosine = jnp.cos(angle)
    sine = jnp.sin(angle)
    upper = jnp.stack([cosine, sine], axis=2)
    lower = jnp.stack([-sine, cosine], axis=2)
    table = jnp.stack([upper, lower], axis=1)
    return table.reshape(2 * nlat, 2 * nlat).astype(jnp.bfloat16)


def spectra_kernel(
    bands,
    slots,
    entry_ref,
    source_ref,
    order_ref,
    keep_ref,
    last_ref,
    has_ref,
    weight_ref,
    field_ref,
    table_ref,
    grid_ref,
    spectra_ref,
    send_ref,
    recv_a_ref,
    recv_b_ref,
    sums_ref,
    out_ref,
    send_sem,
    recv_sem,
    out_sem,
    in_sem,
):
    me = lax.axis_index("band")
    recv_refs = (recv_a_ref, recv_b_ref)
    width = recv_a_ref.shape[-1]
    pixels = recv_a_ref.shape[-2]
    rows = spectra_ref.shape[-2]
    scale = 1.0 / math.sqrt(NLON)

    def partner(k):
        return lax.rem(me + bands // 2 + (k // 2) * (1 - 2 * lax.rem(k, 2)), bands)

    def block_copy(part, other, slot):
        return pltpu.make_async_remote_copy(
            src_ref=send_ref.at[part, other],
            dst_ref=recv_refs[part].at[slot],
            send_sem=send_sem.at[part, other],
            recv_sem=recv_sem.at[part, slot],
            device_id={"band": other},
            device_id_type=pl.DeviceIdType.MESH,
        )

    def spectrum_copy(part, other, slot):
        return pltpu.make_async_remote_copy(
            src_ref=out_ref.at[part, other],
            dst_ref=spectra_ref.at[part, slot],
            send_sem=out_sem.at[part, other],
            recv_sem=in_sem.at[part, slot],
            device_id={"band": other},
            device_id_type=pl.DeviceIdType.MESH,
        )

    def loop(body):
        def step(k, carry):
            body(partner(k))
            return carry

        lax.fori_loop(1, bands, step, 0)

    barrier = pltpu.get_barrier_semaphore()
    loop(
        lambda other: pl.semaphore_signal(
            barrier, inc=1, device_id={"band": other}, device_id_type=pl.DeviceIdType.MESH
        )
    )

    def product(part, other, slot):
        at = other * slots + slot
        block = field_ref[source_ref[at]][:, part * width : (part + 1) * width]
        return jnp.dot(
            weight_ref[entry_ref[at]], block, preferred_element_type=jnp.float32
        ).astype(jnp.bfloat16)

    pl.semaphore_wait(barrier, bands - 1)
    for part in range(CHUNKS):

        def make(other):
            for slot in range(slots):
                send_ref[part, other, slot] = product(part, other, slot)
            block_copy(part, other, me).start()

        loop(make)
        for slot in range(slots):
            recv_refs[part][me, slot] = product(part, me, slot)

    for part in range(CHUNKS):
        lanes = slice(part * width, (part + 1) * width)
        loop(lambda other: block_copy(part, other, other).wait_recv())

        def add(j, run):
            at = order_ref[j]
            run = run * keep_ref[j] + recv_refs[part][at // slots, lax.rem(at, slots)].astype(
                jnp.float32
            )
            sums_ref[part, j] = run.astype(jnp.bfloat16)
            return run

        lax.fori_loop(0, bands * slots, add, jnp.zeros((pixels, width), jnp.float32))

        def place(t, carry):
            block = sums_ref[part, last_ref[t]].astype(jnp.float32) * has_ref[t]
            start = pl.multiple_of(t * pixels, pixels)
            grid_ref[pl.ds(start, pixels), lanes] = block.astype(jnp.bfloat16)
            return carry

        lax.fori_loop(0, TB_DEV, place, 0)
        for lat in range(LAT_DEV):
            spectrum = jnp.dot(
                table_ref[...],
                grid_ref[lat * NLON : (lat + 1) * NLON, lanes],
                preferred_element_type=jnp.float32,
            )
            spectrum = (spectrum * scale).astype(jnp.bfloat16)
            out_ref[part, :, lat] = spectrum.reshape(bands, rows, width)
        loop(lambda other: spectrum_copy(part, other, me).start())
        spectra_ref[part, me] = out_ref[part, me]

    for part in range(CHUNKS):
        loop(lambda other: spectrum_copy(part, other, other).wait_recv())
        loop(lambda other: spectrum_copy(part, other, me).wait_send())
        loop(lambda other: block_copy(part, other, me).wait_send())


def spectra_of_bands(scalars, weight, field, table, bands, slots, rows):
    pixels = field.shape[1]
    width = field.shape[2] // CHUNKS
    blocks = (CHUNKS, bands, slots, pixels, width)
    spectra = (CHUNKS, bands, LAT_DEV, rows, width)
    smem = pl.BlockSpec(memory_space=pltpu.SMEM)
    vmem = pl.BlockSpec(memory_space=pltpu.VMEM)
    dma = pltpu.SemaphoreType.DMA((CHUNKS, bands))
    return pl.pallas_call(
        lambda *refs: spectra_kernel(bands, slots, *refs),
        out_shape=(
            jax.ShapeDtypeStruct((LAT_DEV * NLON, field.shape[2]), jnp.bfloat16),
            jax.ShapeDtypeStruct(spectra, jnp.bfloat16),
        ),
        in_specs=[smem] * len(scalars) + [vmem] * 3,
        out_specs=(vmem, vmem),
        scratch_shapes=[
            pltpu.VMEM(blocks, jnp.bfloat16),
            pltpu.VMEM(blocks[1:], jnp.bfloat16),
            pltpu.VMEM(blocks[1:], jnp.bfloat16),
            pltpu.VMEM((CHUNKS, bands * slots, pixels, width), jnp.bfloat16),
            pltpu.VMEM(spectra, jnp.bfloat16),
            dma,
            dma,
            dma,
            dma,
        ],
        compiler_params=pltpu.CompilerParams(
            collective_id=0, has_side_effects=True, vmem_limit_bytes=56 * 2**20
        ),
        name="spectra_of_bands",
    )(*scalars, weight, field, table)


def per_device(
    source_field,
    interp_weight,
    dest_band,
    target_block,
    source_block,
    entry_count,
    mode_index,
    filter_weight,
):
    bands = lax.axis_size("band")
    entries = interp_weight.shape[0]
    slots = max(2, 3 * entries // (2 * bands))
    total_slots = bands * slots
    channels = source_field.shape[2]
    width = channels // CHUNKS
    modes = mode_index.shape[0]
    mode_dev = modes // bands
    nlat = LAT_DEV * bands

    entry_ids = jnp.arange(entries, dtype=jnp.int32)
    dest = dest_band[:, 0]
    valid = entry_ids < entry_count[0]

    earlier = (dest[:, None] == dest[None, :]) & (entry_ids[:, None] > entry_ids[None, :])
    rank = jnp.sum(earlier.astype(jnp.int32), axis=1)
    position = dest * slots + rank
    slot_ids = jnp.arange(total_slots, dtype=jnp.int32)
    placed = slot_ids[:, None] == position[None, :]
    entry_of = jnp.sum(jnp.where(placed, entry_ids[None, :], 0), axis=1)
    source_of = jnp.sum(jnp.where(placed, source_block[None, :], 0), axis=1)
    target_of = jnp.max(
        jnp.where(placed & valid[None, :], target_block[None, :], -1), axis=1
    ).reshape(bands, slots)

    ids = lax.all_to_all(target_of, "band", split_axis=0, concat_axis=0, tiled=True)
    ids = ids.reshape(total_slots)
    ids = jnp.where(ids < 0, TB_DEV, ids)
    keys = ids * total_slots + slot_ids
    rank = jnp.sum((keys[None, :] < keys[:, None]).astype(jnp.int32), axis=1)
    at_rank = rank[None, :] == slot_ids[:, None]
    order = jnp.sum(jnp.where(at_rank, slot_ids[None, :], 0), axis=1)
    before = jnp.sum((rank[None, :] + 1 == slot_ids[:, None]) * (ids + 1)[None, :], axis=1)
    here = jnp.sum(jnp.where(at_rank, (ids + 1)[None, :], 0), axis=1)
    keep = (before == here).astype(jnp.float32)
    blocks = jnp.arange(TB_DEV, dtype=jnp.int32)
    last = jnp.maximum(jnp.sum((ids[None, :] <= blocks[:, None]).astype(jnp.int32), axis=1) - 1, 0)
    has = jnp.max((ids[None, :] == blocks[:, None]).astype(jnp.float32), axis=1)

    rows = -(-2 * mode_dev // 16) * 16
    forward = lon_table(mode_index, bands, rows)
    scalars = (entry_of, source_of, order, keep, last, has)
    regridded, spectra = spectra_of_bands(
        scalars, interp_weight, source_field, forward, bands, slots, rows
    )

    pencils = spectra.reshape(CHUNKS, nlat, rows, width)[:, :, : 2 * mode_dev]
    pencils = pencils.reshape(CHUNKS, 2 * nlat, mode_dev, width)
    table = lat_table(nlat)
    filt = filter_weight.astype(jnp.float32)
    factor = jnp.where((mode_index == 0) | (mode_index == NLON // 2), 1.0, 2.0).astype(jnp.float32)
    factor = lax.dynamic_slice_in_dim(factor, lax.axis_index("band") * mode_dev, mode_dev)
    mixed = jnp.einsum(
        "ab,hbmc->amhc", table, pencils, preferred_element_type=jnp.float32
    ) * (1.0 / math.sqrt(nlat))
    mixed = mixed.reshape(nlat, 2, mode_dev, channels)
    real_part = filt[:, 0] * mixed[:, 0] - filt[:, 1] * mixed[:, 1]
    imag_part = filt[:, 0] * mixed[:, 1] + filt[:, 1] * mixed[:, 0]
    shaped = (
        jnp.stack([real_part, imag_part], axis=1)
        .astype(jnp.bfloat16)
        .reshape(2 * nlat, mode_dev * channels)
    )
    back = lax.dot_general(
        table, shaped, (((0,), (0,)), ((), ())), preferred_element_type=jnp.float32
    ) * (1.0 / math.sqrt(nlat))
    back = back.reshape(nlat, 2, mode_dev, channels) * factor[None, None, :, None]
    back = back.astype(jnp.bfloat16).reshape(bands, LAT_DEV, 2 * mode_dev, channels)
    back = lax.all_to_all(back, "band", split_axis=0, concat_axis=0, tiled=True)
    returned = back.transpose(1, 0, 2, 3).reshape(LAT_DEV, 2 * modes, channels)
    inverse = forward.reshape(bands, rows, NLON)[:, : 2 * mode_dev].reshape(2 * modes, NLON)
    filtered = jnp.einsum(
        "lkc,kn->lnc", returned, inverse, preferred_element_type=jnp.float32
    ) * (1.0 / math.sqrt(NLON))
    regridded = regridded.reshape(LAT_DEV, NLON, channels)
    processed = (regridded.astype(jnp.float32) + filtered).astype(jnp.bfloat16)
    return processed.reshape(LAT_DEV * NLON, channels)


def solution(mesh):
    in_specs = (
        P(("grp", "band"), None, None),
        P("band", None, None),
        P("band", None),
        P("band"),
        P("band"),
        P("band"),
        P(),
        P(None, None, "band", None),
    )
    out_specs = P(("grp", "band"), None)
    return jax.shard_map(
        per_device, mesh=mesh, in_specs=in_specs, out_specs=out_specs, check_vma=False
    )
```

time: 399 us -> 369 us (0.925)
  Pallas kernels: 0 us -> 246 us
  waiting for transfers between devices: 181 us -> 0.01 us
  starting transfers between devices: 54 us -> 7.35 us
  local copies, waits for them, and re-layouts: 72.7 us -> 36 us
  matrix products: 23.9 us -> 6.81 us
  other arithmetic: 20.2 us -> 27.2 us
    pallas_call x0 -> x1, Pallas kernels: none -> 246 us  [spectra_of_bands(): pl.pallas_call(lambda *refs: spectra_kernel(bands, slots, *refs), out_sha...]
    all_to_all x3 -> x1, waiting for transfers between devices: 181 us -> 0.01 us  [per_device(): lax.all_to_all(target_of, 'band', split_axis=0, concat_axis=0, tiled=True)]
    all_to_all x3 -> x1, starting transfers between devices: 54 us -> 7.35 us  [per_device(): lax.all_to_all(target_of, 'band', split_axis=0, concat_axis=0, tiled=True)]
    scatter x2 -> x0, local copies, waits for them, and re-layouts: 18.7 us -> none  [the longest x1 17.7 us: per_device(): jnp.zeros((total_slots, pixels, channels), jnp.bfloat16).at[position]]
    unnamed x19 -> x9, local copies, waits for them, and re-layouts: 19.2 us -> 1.94 us
    dot_general x5 -> x2, matrix products: 23.3 us -> 6.21 us  [the longest x1 4.19 us: per_device(): jnp.einsum('lkc,kn->lnc', returned, inverse, preferred_element_type=jnp.f...]
    another operation x5 -> x3, other arithmetic: 12.2 us -> 2.67 us
    sub x0 -> x1, other arithmetic: none -> 7.92 us  [lon_table(): cos_high * cos_low - sin_high * sin_low]
  transfers between devices with their start and end apart: 3 -> 1, of which waited for: 2 -> 0; matrix products, arithmetic and copies ran while one was open for 17% -> 10% of each run, Pallas kernels for 0% -> 0%
where the time goes in v2:
time: 369 us; the launch traced here: 368 us
  Pallas kernels  246 us (67%)
  blocking collectives  43.6 us (12%)
  local copies, waits for them, and re-layouts  36 us (10%)
  other arithmetic  27.2 us (7%)
  starting transfers between devices  7.35 us (2%)
  matrix products  6.81 us (2%)
    pallas_call x1, Pallas kernels, spectra_of_bands(): pl.pallas_call(lambda *refs: spectra_kernel(bands, slots, *refs), out_sha...  246 us
    all_to_all x1, blocking collectives, per_device(): back = lax.all_to_all(back, 'band', split_axis=0, concat_axis=0, tiled=True)  43.6 us
    sub x1, other arithmetic, lon_table(): cos_high * cos_low - sin_high * sin_low  7.92 us
  transfers between devices with their start and end apart: 1, of which 0 were waited for; matrix products, arithmetic and copies ran while one was open for 10% of the time, Pallas kernels for 0%

profile of v2, /device:TPU:1, one launch (start us, length us, event | category | flops | bytes accessed | tf_op | source)
XLA Modules:
  0.0 368.1 jit_solution(1102281775062423095)
XLA Ops:
  0.0 0.9 convert_reduce_fusion.3
  0.9 0.7 multiply_add_fusion
  2.2 1.4 select_reduce_fusion.3
  3.7 0.7 all_to_all.9
  4.4 7.3 %all-to-all-start = ((s32[16,1,9]{2,1,0:T(1,128)}), s32[16,1,9]{2,1,0:T(1,128)S(1)}, u32[]{:S(2)}, u32[]{:S(2)}) async-start(s32[16,1,9]{2,1,0:T(1,128)} %bitcast.2), calls=%async_computation | async-start | bytes 16384 | tf_op jit(solution)/shard_map/all_to_all | solution.py:243
  11.7 0.1 fusion.26
  11.9 0.2 negate_convert_fusion
  12.0 1.6 fusion.9
  13.6 0.7 or_select_fusion
  14.3 1.6 fusion.13
  15.9 7.9 %multiply_subtract_fusion = (bf16[384,40,36]{2,1,0:T(8,128)(2,1)}, bf16[384,40,36]{2,1,0:T(8,128)(2,1)}) fusion(f32[384,36]{1,0:T(8,128)S(1)} %get-tuple-element.24, f32[384,40]{1,0:T(8,128)S(1)} %get-tuple-element.22, f32[384,36]{1,0:T(8,128)S(1)} %get-tuple-element.23, f32[384,40]{1,0:T(8,128)S(1)} %get-tuple-element.21), kind=kLoop, calls=%fused_computation.1 | loop fusion | flops 4976640 | bytes 2445312 | tf_op jit(solution)/shard_map/sub | solution.py:29
  23.8 5.2 %neg.25 = bf16[16,1,24,1440]{3,2,0,1:T(8,128)(2,1)S(1)} reshape(bf16[384,40,36]{2,1,0:T(8,128)(2,1)} %get-tuple-element.18) | data formatting | bytes 2211840 | tf_op jit(solution)/shard_map/neg | solution.py:31
  29.0 5.2 %sub.23 = bf16[16,1,24,1440]{3,2,0,1:T(8,128)(2,1)S(1)} reshape(bf16[384,40,36]{2,1,0:T(8,128)(2,1)} %get-tuple-element.17) | data formatting | bytes 2211840 | tf_op jit(solution)/shard_map/sub | solution.py:29
  34.2 1.6 maximum_convert_fusion
  35.9 1.1 copy.25
  37.0 3.2 convert_element_type.127
  40.1 3.2 reshape.403
  43.3 0.0 copy-start.2
  43.3 3.5 copy.24
  46.8 0.0 copy-done.2
  46.8 2.1 convert_element_type.128
  48.9 0.1 dynamic_slice.3
  49.0 0.1 mul.357
  49.1 0.0 all-to-all-done
  49.1 0.5 broadcast.330
  49.6 0.7 reduce.3
  50.3 0.1 reshape.397
  50.4 0.1 convert_reduce_fusion.2
  50.5 0.7 convert_reduce_fusion.1.refs_5_
  51.1 0.2 convert_reduce_fusion
  51.3 0.6 add_maximum_fusion.refs_4_
  51.9 0.7 select_reduce_fusion
  52.6 0.6 compare_convert_fusion.refs_3_
  53.2 246.3 %spectra_of_bands.1 = (bf16[5760,256]{1,0:T(8,128)(2,1)}, bf16[2,16,4,48,128]{4,3,2,1,0:T(8,128)(2,1)}) custom-call(s32[144]{0:T(256)} %get-tuple-element.14.refs_0_, s32[144]{0:T(256)} %get-tuple-element.13.refs_1_, s32[144]{0:T(256)} %get-tuple-element.10.refs_2_, f32[144]{0:T(256)} %compare_convert_fusion.refs_3_, s32[45]{0:T(128)} %add_maximum_fusion.refs_4_, ...), custom_call_target="tpu_custom_call" | custom-call | tf_op jit(solution)/shard_map/spectra_of_bands/pallas_call | solution.py:182
  299.5 2.0 multiply_bitcast_fusion
  301.6 3.6 copy.27
  305.1 5.7 %reshape.398 = f32[64,2,24,256]{3,2,1,0:T(8,128)} reshape(f32[128,24,2,128]{3,2,1,0:T(2,128)} %copy.27) | data formatting | bytes 6291456 | tf_op jit(solution)/shard_map/reshape | solution.py:273
  310.8 0.0 copy-done
  310.8 2.4 subtract_convert_fusion
  313.2 0.1 pad_maximum_fusion
  313.3 0.4 copy.30
  313.7 0.6 convolution_multiply_fusion
  314.3 1.9 reshape.399
  316.3 2.3 multiply_convert_fusion
  318.6 43.6 %all_to_all.14 = bf16[16,4,48,256]{3,2,1,0:T(8,128)(2,1)S(1)} all-to-all(bf16[16,4,48,256]{3,2,1,0:T(8,128)(2,1)S(1)} %multiply_convert_fusion), channel_id=1, replica_groups=mesh['grp'=2,'band'=16] {'band'}, dimensions={0} | all-to-all | bytes 3145728 | tf_op jit(solution)/shard_map/all_to_all | solution.py:286
  362.2 0.1 copy.28
  362.4 1.5 copy-done.1
  363.9 4.2 %fusion = bf16[4,1440,256]{2,1,0:T(8,128)(2,1)} fusion(bf16[4,1440,256]{2,1,0:T(8,128)(2,1)S(1)} %bitcast.43, bf16[768,1440,1]{1,0,2:T(8,128)(2,1)S(1)} %bitcast.37, bf16[4,768,256]{2,1,0:T(8,128)(2,1)S(1)} %bitcast.42), kind=kOutput, calls=%fused_computation.4 | convolution fusion | flops 2270822400 | bytes 9682944 | tf_op jit(solution)/shard_map/lkc,kn->lnc/dot_general | solution.py:289
  (11 shorter events, 0.1 us)
Async XLA Ops:
  4.4 44.7 %all-to-all-start = ((s32[16,1,9]{2,1,0:T(1,128)}), s32[16,1,9]{2,1,0:T(1,128)S(1)}, u32[]{:S(2)}, u32[]{:S(2)}) async-start(s32[16,1,9]{2,1,0:T(1,128)} %bitcast.2), calls=%async_computation | async-start | bytes 16384 | tf_op jit(solution)/shard_map/all_to_all | solution.py:243
  43.3 3.5 copy-start.2
  305.1 5.7 %copy-start = (f32[64,2,24,256]{3,2,1,0:T(8,128)S(1)}, f32[64,2,24,256]{3,2,1,0:T(8,128)}, u32[]{:S(2)}) copy-start(f32[64,2,24,256]{3,2,1,0:T(8,128)} %convert_element_type.128) | copy-start | bytes 9437188
  318.6 43.8 %copy-start.3 = (bf16[5760,256]{1,0:T(8,128)(2,1)S(1)}, bf16[5760,256]{1,0:T(8,128)(2,1)}, u32[]{:S(2)}) copy-start(bf16[5760,256]{1,0:T(8,128)(2,1)} %get-tuple-element.7) | copy-start | bytes 8847364
  362.2 1.7 copy-start.1

commit v3 on v2

v3 whole, which is shorter than its diff:
```python
import math

import jax
import jax.numpy as jnp
from jax import lax
from jax.experimental import pallas as pl
from jax.experimental.pallas import tpu as pltpu
from jax.sharding import PartitionSpec as P

NLON = 1440
LAT_DEV = 4
TB_DEV = 45
CHUNKS = 2
LANES = 128
ROW_STEP = 32
GROUP = 6


def waves(phase, period):
    angle = (phase % period).astype(jnp.float32) * (2.0 * math.pi / period)
    return jnp.cos(angle), jnp.sin(angle)


def lon_parts(mode_index, bands, rows):
    per_band = mode_index.shape[0] // bands
    mode = jnp.broadcast_to(mode_index.reshape(bands, 1, per_band), (bands, 2, per_band))
    mode = mode.reshape(bands, 2 * per_band)
    mode = jnp.pad(mode, ((0, 0), (0, rows - 2 * per_band))).reshape(bands * rows)
    real = jnp.arange(bands * rows, dtype=jnp.int32) % rows < per_band
    outs = []
    for step, along in ((LANES, 1), (ROW_STEP, 0)):
        high = jnp.arange(0, NLON, step, dtype=jnp.int32)
        low = jnp.arange(step, dtype=jnp.int32)
        pick = jnp.expand_dims(real, along)
        modes = jnp.expand_dims(mode, along)
        cos_high, sin_high = waves(modes * jnp.expand_dims(high, 1 - along), NLON)
        cos_low, sin_low = waves(modes * jnp.expand_dims(low, 1 - along), NLON)
        outer = jnp.where(pick, cos_high, -sin_high)
        inner = jnp.where(pick, -sin_high, -cos_high)
        outs += [outer, inner, cos_low, sin_low]
    return outs


def lat_tables(nlat):
    index = jnp.arange(nlat, dtype=jnp.int32)
    cosine, sine = waves(index[:, None] * index[None, :], nlat)
    upper = jnp.concatenate([cosine, sine], axis=1)
    lower = jnp.concatenate([-sine, cosine], axis=1)
    turned = jnp.concatenate([cosine, -sine], axis=1)
    table = jnp.concatenate([upper, lower], axis=0).astype(jnp.bfloat16)
    flipped = jnp.concatenate(
        [turned, jnp.concatenate([sine, cosine], axis=1)], axis=0
    ).astype(jnp.bfloat16)
    return table, flipped


def layer_kernel(
    bands,
    slots,
    entry_ref,
    source_ref,
    order_ref,
    keep_ref,
    last_ref,
    has_ref,
    factor_ref,
    weight_ref,
    field_ref,
    filter_ref,
    outer_ref,
    inner_ref,
    cos_low_ref,
    sin_low_ref,
    outer_row_ref,
    inner_row_ref,
    cos_row_ref,
    sin_row_ref,
    lat_ref,
    lat_flipped_ref,
    out_ref,
    send_a_ref,
    send_b_ref,
    recv_a_ref,
    recv_b_ref,
    table_ref,
    inverse_ref,
    filter_f32_ref,
    spec_send_ref,
    spec_recv_ref,
    back_send_ref,
    back_recv_ref,
    mode_ref,
    shaped_ref,
    send_sem,
    recv_sem,
    spec_send_sem,
    spec_recv_sem,
    back_send_sem,
    back_recv_sem,
):
    me = lax.axis_index("band")
    send_refs = (send_a_ref, send_b_ref)
    recv_refs = (recv_a_ref, recv_b_ref)
    width = recv_a_ref.shape[-1]
    pixels = recv_a_ref.shape[-2]
    rows = spec_recv_ref.shape[-2]
    nlat = LAT_DEV * bands
    mode_dev = filter_ref.shape[2]
    filter_total = filter_f32_ref.shape[0] // CHUNKS
    filter_rows = filter_total // (2 * nlat)
    lon_scale = 1.0 / math.sqrt(NLON)
    lat_scale = 1.0 / math.sqrt(nlat)

    def partner(k):
        return lax.rem(me + bands // 2 + (k // 2) * (1 - 2 * lax.rem(k, 2)), bands)

    def remote(source, goal, out_sem, in_sem, part, other, slot):
        return pltpu.make_async_remote_copy(
            src_ref=source.at[other],
            dst_ref=goal.at[slot],
            send_sem=out_sem.at[part, other],
            recv_sem=in_sem.at[part, slot],
            device_id={"band": other},
            device_id_type=pl.DeviceIdType.MESH,
        )

    def block_copy(part, other, slot):
        return remote(send_refs[part], recv_refs[part], send_sem, recv_sem, part, other, slot)

    def spectrum_copy(part, other, slot):
        return remote(
            spec_send_ref.at[part],
            spec_recv_ref.at[part],
            spec_send_sem,
            spec_recv_sem,
            part,
            other,
            slot,
        )

    def back_copy(part, other, slot):
        return remote(
            back_send_ref.at[part],
            back_recv_ref.at[part],
            back_send_sem,
            back_recv_sem,
            part,
            other,
            slot,
        )

    def loop(body):
        def step(k, carry):
            body(partner(k))
            return carry

        lax.fori_loop(1, bands, step, 0)

    barrier = pltpu.get_barrier_semaphore()
    loop(
        lambda other: pl.semaphore_signal(
            barrier, inc=1, device_id={"band": other}, device_id_type=pl.DeviceIdType.MESH
        )
    )

    def product(part, other, slot):
        at = other * slots + slot
        block = field_ref[source_ref[at]][:, part * width : (part + 1) * width]
        return jnp.dot(
            weight_ref[entry_ref[at]], block, preferred_element_type=jnp.float32
        ).astype(jnp.bfloat16)

    pl.semaphore_wait(barrier, bands - 1)
    for part in range(CHUNKS):

        def make(other):
            for slot in range(slots):
                send_refs[part][other, slot] = product(part, other, slot)
            block_copy(part, other, me).start()

        loop(make)
        for slot in range(slots):
            recv_refs[part][me, slot] = product(part, me, slot)

    for first in range(0, NLON, LANES):
        span = min(LANES, NLON - first)
        at = first // LANES
        table_ref[:, first : first + span] = (
            outer_ref[:, at : at + 1] * cos_low_ref[:, :span]
            + inner_ref[:, at : at + 1] * sin_low_ref[:, :span]
        ).astype(jnp.bfloat16)
    for first in range(0, NLON, ROW_STEP):
        at = first // ROW_STEP
        inverse_ref[first : first + ROW_STEP, :] = (
            outer_row_ref[at : at + 1, :] * cos_row_ref[...]
            + inner_row_ref[at : at + 1, :] * sin_row_ref[...]
        ).astype(jnp.bfloat16)

    def widen(lat, carry):
        for half in range(2):
            start = pl.multiple_of((lat * 2 + half) * filter_rows, 8)
            block = filter_ref[lat, half].astype(jnp.float32)
            for part in range(CHUNKS):
                filter_f32_ref[pl.ds(part * filter_total + start, mode_dev), :] = block[
                    :, part * width : (part + 1) * width
                ]
        return carry

    lax.fori_loop(0, nlat, widen, 0)
    if rows > 2 * mode_dev:
        shaped_ref[...] = jnp.zeros_like(shaped_ref)

    for part in range(CHUNKS):
        lanes = slice(part * width, (part + 1) * width)
        sums_ref = send_refs[part]
        loop(lambda other: block_copy(part, other, other).wait_recv())
        loop(lambda other: block_copy(part, other, me).wait_send())

        def add(j, run):
            at = order_ref[j]
            run = run * keep_ref[j] + recv_refs[part][at // slots, lax.rem(at, slots)].astype(
                jnp.float32
            )
            sums_ref[j // slots, lax.rem(j, slots)] = run.astype(jnp.bfloat16)
            return run

        lax.fori_loop(0, bands * slots, add, jnp.zeros((pixels, width), jnp.float32))

        def place(t, carry):
            at = last_ref[t]
            block = sums_ref[at // slots, lax.rem(at, slots)].astype(jnp.float32) * has_ref[t]
            start = pl.multiple_of(t * pixels, pixels)
            out_ref[pl.ds(start, pixels), lanes] = block.astype(jnp.bfloat16)
            return carry

        lax.fori_loop(0, TB_DEV, place, 0)
        for lat in range(LAT_DEV):
            spectrum = jnp.dot(
                table_ref[...],
                out_ref[lat * NLON : (lat + 1) * NLON, lanes],
                preferred_element_type=jnp.float32,
            )
            spectrum = (spectrum * lon_scale).astype(jnp.bfloat16)
            spec_send_ref[part, :, lat] = spectrum.reshape(bands, rows, width)
        loop(lambda other: spectrum_copy(part, other, me).start())
        spec_recv_ref[part, me] = spec_send_ref[part, me]

    for part in range(CHUNKS):
        loop(lambda other: spectrum_copy(part, other, other).wait_recv())

        def spread(band, carry):
            start = pl.multiple_of(band * LAT_DEV * rows, LAT_DEV * rows)
            block = spec_recv_ref[part, band].astype(jnp.float32)
            mode_ref[pl.ds(start, LAT_DEV * rows), :] = block.reshape(LAT_DEV * rows, width)
            return carry

        lax.fori_loop(0, bands, spread, 0)

        def mix(group, carry):
            columns = []
            for i in range(GROUP):
                mode = group * GROUP + i
                halves = [
                    mode_ref[pl.ds(half * mode_dev + mode, nlat, stride=rows), :]
                    for half in range(2)
                ]
                columns.append(jnp.concatenate(halves, axis=0).astype(jnp.bfloat16))
            mixed = (
                jnp.dot(
                    lat_ref[...],
                    jnp.concatenate(columns, axis=1),
                    preferred_element_type=jnp.float32,
                )
                * lat_scale
            )
            columns = []
            for i in range(GROUP):
                mode = group * GROUP + i
                own = mixed[:, i * width : (i + 1) * width]
                gain = [
                    filter_f32_ref[
                        pl.ds(
                            part * filter_total + half * filter_rows + mode,
                            nlat,
                            stride=2 * filter_rows,
                        ),
                        :,
                    ]
                    for half in range(2)
                ]
                real, imag = own[:nlat], own[nlat:]
                shaped = jnp.concatenate(
                    [gain[0] * real - gain[1] * imag, gain[0] * imag + gain[1] * real], axis=0
                )
                columns.append(shaped.astype(jnp.bfloat16))
            back = (
                jnp.dot(
                    lat_flipped_ref[...],
                    jnp.concatenate(columns, axis=1),
                    preferred_element_type=jnp.float32,
                )
                * lat_scale
            )
            for i in range(GROUP):
                mode = group * GROUP + i
                own = back[:, i * width : (i + 1) * width] * factor_ref[mode]
                for half in range(2):
                    shaped_ref[pl.ds(half * mode_dev + mode, nlat, stride=rows), :] = own[
                        half * nlat : (half + 1) * nlat
                    ]
            return carry

        lax.fori_loop(0, mode_dev // GROUP, mix, 0)

        def back_block(band):
            start = pl.multiple_of(band * LAT_DEV * rows, LAT_DEV * rows)
            block = shaped_ref[pl.ds(start, LAT_DEV * rows), :].astype(jnp.bfloat16)
            return block.reshape(LAT_DEV, rows, width)

        def give_back(other):
            back_send_ref[part, other] = back_block(other)
            back_copy(part, other, me).start()

        loop(give_back)
        back_recv_ref[part, me] = back_block(me)

    for part in range(CHUNKS):
        lanes = slice(part * width, (part + 1) * width)
        loop(lambda other: back_copy(part, other, other).wait_recv())
        for lat in range(LAT_DEV):
            filtered = jnp.dot(
                inverse_ref[...],
                back_recv_ref[part, :, lat].reshape(bands * rows, width),
                preferred_element_type=jnp.float32,
            )
            span = slice(lat * NLON, (lat + 1) * NLON)
            out_ref[span, lanes] = (
                out_ref[span, lanes].astype(jnp.float32) + filtered * lon_scale
            ).astype(jnp.bfloat16)
        loop(lambda other: spectrum_copy(part, other, me).wait_send())
        loop(lambda other: back_copy(part, other, me).wait_send())


def layer(scalars, tensors, bands, slots, rows):
    field, filters = tensors[1], tensors[2]
    pixels = field.shape[1]
    width = field.shape[2] // CHUNKS
    nlat, _, mode_dev, channels = filters.shape
    blocks = pltpu.VMEM((bands, slots, pixels, width), jnp.bfloat16)
    spectra = pltpu.VMEM((CHUNKS, bands, LAT_DEV, rows, width), jnp.bfloat16)
    filter_rows = -(-mode_dev // 8) * 8
    smem = pl.BlockSpec(memory_space=pltpu.SMEM)
    vmem = pl.BlockSpec(memory_space=pltpu.VMEM)
    return pl.pallas_call(
        lambda *refs: layer_kernel(bands, slots, *refs),
        out_shape=jax.ShapeDtypeStruct((LAT_DEV * NLON, channels), jnp.bfloat16),
        in_specs=[smem] * len(scalars) + [vmem] * len(tensors),
        out_specs=vmem,
        scratch_shapes=[
            blocks,
            blocks,
            blocks,
            blocks,
            pltpu.VMEM((bands * rows, NLON), jnp.bfloat16),
            pltpu.VMEM((NLON, bands * rows), jnp.bfloat16),
            pltpu.VMEM((CHUNKS * nlat * 2 * filter_rows, width), jnp.float32),
            spectra,
            spectra,
            spectra,
            spectra,
            pltpu.VMEM((nlat * rows, width), jnp.float32),
            pltpu.VMEM((nlat * rows, width), jnp.float32),
        ]
        + [pltpu.SemaphoreType.DMA((CHUNKS, bands))] * 6,
        compiler_params=pltpu.CompilerParams(
            collective_id=0, has_side_effects=True, vmem_limit_bytes=60 * 2**20
        ),
        name="layer",
    )(*scalars, *tensors)


def per_device(
    source_field,
    interp_weight,
    dest_band,
    target_block,
    source_block,
    entry_count,
    mode_index,
    filter_weight,
):
    bands = lax.axis_size("band")
    entries = interp_weight.shape[0]
    slots = max(2, 3 * entries // (2 * bands))
    total_slots = bands * slots
    mode_dev = mode_index.shape[0] // bands
    nlat = LAT_DEV * bands

    entry_ids = jnp.arange(entries, dtype=jnp.int32)
    dest = dest_band[:, 0]
    valid = entry_ids < entry_count[0]

    earlier = (dest[:, None] == dest[None, :]) & (entry_ids[:, None] > entry_ids[None, :])
    rank = jnp.sum(earlier.astype(jnp.int32), axis=1)
    position = dest * slots + rank
    slot_ids = jnp.arange(total_slots, dtype=jnp.int32)
    placed = slot_ids[:, None] == position[None, :]
    entry_of = jnp.sum(jnp.where(placed, entry_ids[None, :], 0), axis=1)
    source_of = jnp.sum(jnp.where(placed, source_block[None, :], 0), axis=1)
    target_of = jnp.max(
        jnp.where(placed & valid[None, :], target_block[None, :], -1), axis=1
    ).reshape(bands, slots)

    ids = lax.all_to_all(target_of, "band", split_axis=0, concat_axis=0, tiled=True)
    ids = ids.reshape(total_slots)
    ids = jnp.where(ids < 0, TB_DEV, ids)
    keys = ids * total_slots + slot_ids
    rank = jnp.sum((keys[None, :] < keys[:, None]).astype(jnp.int32), axis=1)
    at_rank = rank[None, :] == slot_ids[:, None]
    order = jnp.sum(jnp.where(at_rank, slot_ids[None, :], 0), axis=1)
    before = jnp.sum((rank[None, :] + 1 == slot_ids[:, None]) * (ids + 1)[None, :], axis=1)
    here = jnp.sum(jnp.where(at_rank, (ids + 1)[None, :], 0), axis=1)
    keep = (before == here).astype(jnp.float32)
    blocks = jnp.arange(TB_DEV, dtype=jnp.int32)
    last = jnp.maximum(jnp.sum((ids[None, :] <= blocks[:, None]).astype(jnp.int32), axis=1) - 1, 0)
    has = jnp.max((ids[None, :] == blocks[:, None]).astype(jnp.float32), axis=1)

    rows = -(-2 * mode_dev // 16) * 16
    factor = jnp.where((mode_index == 0) | (mode_index == NLON // 2), 1.0, 2.0).astype(jnp.float32)
    factor = lax.dynamic_slice_in_dim(factor, lax.axis_index("band") * mode_dev, mode_dev)
    scalars = (entry_of, source_of, order, keep, last, has, factor)
    tensors = (
        interp_weight,
        source_field,
        filter_weight,
        *lon_parts(mode_index, bands, rows),
        *lat_tables(nlat),
    )
    return layer(scalars, tensors, bands, slots, rows)


def solution(mesh):
    in_specs = (
        P(("grp", "band"), None, None),
        P("band", None, None),
        P("band", None),
        P("band"),
        P("band"),
        P("band"),
        P(),
        P(None, None, "band", None),
    )
    out_specs = P(("grp", "band"), None)
    return jax.shard_map(
        per_device, mesh=mesh, in_specs=in_specs, out_specs=out_specs, check_vma=False
    )
```

time: 369 us -> 316 us (0.86)
  blocking collectives: 43.6 us -> 0 us
  Pallas kernels: 246 us -> 283 us
  local copies, waits for them, and re-layouts: 36 us -> 6.37 us
  other arithmetic: 27.2 us -> 16.3 us
  matrix products: 6.81 us -> 0 us
    all_to_all x1 -> x0, blocking collectives: 43.6 us -> none  [per_device(): back = lax.all_to_all(back, 'band', split_axis=0, concat_axis=0, tiled=True)]
    pallas_call x1, Pallas kernels: 246 us -> 283 us  [layer(): pl.pallas_call(lambda *refs: layer_kernel(bands, slots, *refs), out_shape...]
    convert_element_type x3 -> x0, local copies, waits for them, and re-layouts: 9.83 us -> none  [the longest x2 6.31 us: lat_table(): return table.reshape(2 * nlat, 2 * nlat).astype(jnp.bfloat16)]
    sub x1 -> x0, other arithmetic: 7.92 us -> none  [lon_table(): cos_high * cos_low - sin_high * sin_low]
    reshape x2 -> x0, local copies, waits for them, and re-layouts: 7.59 us -> none  [the longest x1 5.68 us: per_device(): mixed = mixed.reshape(nlat, 2, mode_dev, channels)]
    dot_general x3 -> x0, matrix products: 6.81 us -> none  [the longest x1 4.19 us: per_device(): jnp.einsum('lkc,kn->lnc', returned, inverse, preferred_element_type=jnp.f...]
    convert_element_type x3 -> x0, other arithmetic: 6.03 us -> none  [the longest x1 2.32 us: per_device(): back.astype(jnp.bfloat16).reshape(bands, LAT_DEV, 2 * mode_dev, channels)]
    sub x1 -> x0, local copies, waits for them, and re-layouts: 5.2 us -> none  [lon_table(): cos_high * cos_low - sin_high * sin_low]
  transfers between devices with their start and end apart: 1 -> 1, of which waited for: 0 -> 0; matrix products, arithmetic and copies ran while one was open for 10% -> 4% of each run, Pallas kernels for 0% -> 0%
where the time goes in v3:
time: 316 us; the launch traced here: 314 us
  Pallas kernels  283 us (90%)
  other arithmetic  16.3 us (5%)
  starting transfers between devices  7.35 us (2%)
  local copies, waits for them, and re-layouts  6.37 us (2%)
    pallas_call x1, Pallas kernels, layer(): pl.pallas_call(lambda *refs: layer_kernel(bands, slots, *refs), out_shape...  283 us
    all_to_all x1, starting transfers between devices, per_device(): lax.all_to_all(target_of, 'band', split_axis=0, concat_axis=0, tiled=True)  7.35 us
  transfers between devices with their start and end apart: 1, of which 0 were waited for; matrix products, arithmetic and copies ran while one was open for 4% of the time, Pallas kernels for 0%

profile of v3, /device:TPU:1, one launch (start us, length us, event | category | flops | bytes accessed | tf_op | source)
XLA Modules:
  0.0 313.6 jit_solution(17837693452750218003)
XLA Ops:
  0.7 0.9 convert_reduce_fusion.3
  1.6 0.7 multiply_add_fusion
  2.2 1.4 select_reduce_fusion.3
  3.7 0.7 all_to_all.6
  4.4 7.3 %all-to-all-start = ((s32[16,1,9]{2,1,0:T(1,128)}), s32[16,1,9]{2,1,0:T(1,128)S(1)}, u32[]{:S(2)}, u32[]{:S(2)}) async-start(s32[16,1,9]{2,1,0:T(1,128)} %bitcast.2), calls=%async_computation | async-start | bytes 16384 | tf_op jit(solution)/shard_map/all_to_all | solution.py:414
  11.8 0.7 or_select_fusion
  12.4 0.8 broadcast_in_dim.127
  13.2 0.1 fusion.39
  13.4 0.2 negate_convert_fusion
  13.5 0.1 mul.212
  13.6 1.1 fusion.25
  14.7 2.7 fusion.6
  17.4 1.4 negate_select_fusion.1
  18.8 3.0 negate_select_fusion
  21.8 0.7 fusion.31
  22.5 0.6 dynamic_slice.3.refs_6_
  23.2 0.0 all-to-all-done
  23.2 0.5 broadcast.145
  23.6 0.6 reduce.3
  24.2 0.1 reshape.105
  24.3 0.7 convert_reduce_fusion.1.refs_5_
  25.0 0.1 convert_reduce_fusion.2
  25.1 0.2 convert_reduce_fusion
  25.3 0.5 add_maximum_fusion.refs_4_
  25.8 0.7 select_reduce_fusion
  26.5 0.6 compare_convert_fusion.refs_3_
  27.1 282.8 %layer.1 = bf16[5760,256]{1,0:T(8,128)(2,1)} custom-call(s32[144]{0:T(256)} %get-tuple-element.10.refs_0_, s32[144]{0:T(256)} %get-tuple-element.9.refs_1_, s32[144]{0:T(256)} %get-tuple-element.6.refs_2_, f32[144]{0:T(256)} %compare_convert_fusion.refs_3_, s32[45]{0:T(128)} %add_maximum_fusion.refs_4_, f32[45]{0:T(128)} %convert_reduce_fusion.1.refs_5_, ...), custom_call_target="tpu_custom_call" | custom-call | tf_op jit(solution)/shard_map/layer/pallas_call | solution.py:354
  309.9 3.6 %copy.13 = bf16[5760,256]{1,0:T(8,128)(2,1)} copy(bf16[5760,256]{1,0:T(8,128)(2,1)} %layer.1) | data formatting | bytes 5898240
  (7 shorter events, 0.0 us)
Async XLA Ops:
  4.4 18.8 %all-to-all-start = ((s32[16,1,9]{2,1,0:T(1,128)}), s32[16,1,9]{2,1,0:T(1,128)S(1)}, u32[]{:S(2)}, u32[]{:S(2)}) async-start(s32[16,1,9]{2,1,0:T(1,128)} %bitcast.2), calls=%async_computation | async-start | bytes 16384 | tf_op jit(solution)/shard_map/all_to_all | solution.py:414

commit v4 on v3

--- a/solution.py
+++ b/solution.py
@@ -171,17 +171,19 @@
         ).astype(jnp.bfloat16)
 
     pl.semaphore_wait(barrier, bands - 1)
-    for part in range(CHUNKS):
-
+    def make_part(part):
         def make(other):
             for slot in range(slots):
                 send_refs[part][other, slot] = product(part, other, slot)
+            if part > 0:
+                block_copy(part - 1, other, me).wait_send()
             block_copy(part, other, me).start()
 
         loop(make)
         for slot in range(slots):
             recv_refs[part][me, slot] = product(part, me, slot)
 
+    make_part(0)
     for first in range(0, NLON, LANES):
         span = min(LANES, NLON - first)
         at = first // LANES
@@ -210,11 +212,15 @@
     if rows > 2 * mode_dev:
         shaped_ref[...] = jnp.zeros_like(shaped_ref)
 
-    for part in range(CHUNKS):
+    for part in range(1, CHUNKS):
+        make_part(part)
+
+    def to_spectra(part):
         lanes = slice(part * width, (part + 1) * width)
         sums_ref = send_refs[part]
         loop(lambda other: block_copy(part, other, other).wait_recv())
-        loop(lambda other: block_copy(part, other, me).wait_send())
+        if part == CHUNKS - 1:
+            loop(lambda other: block_copy(part, other, me).wait_send())
 
         def add(j, run):
             at = order_ref[j]
@@ -245,7 +251,7 @@
         loop(lambda other: spectrum_copy(part, other, me).start())
         spec_recv_ref[part, me] = spec_send_ref[part, me]
 
-    for part in range(CHUNKS):
+    def to_back(part):
         loop(lambda other: spectrum_copy(part, other, other).wait_recv())
 
         def spread(band, carry):
@@ -324,7 +330,7 @@
         loop(give_back)
         back_recv_ref[part, me] = back_block(me)
 
-    for part in range(CHUNKS):
+    def to_grid(part):
         lanes = slice(part * width, (part + 1) * width)
         loop(lambda other: back_copy(part, other, other).wait_recv())
         for lat in range(LAT_DEV):
@@ -339,6 +345,14 @@
             ).astype(jnp.bfloat16)
         loop(lambda other: spectrum_copy(part, other, me).wait_send())
         loop(lambda other: back_copy(part, other, me).wait_send())
+
+    to_spectra(0)
+    for part in range(1, CHUNKS):
+        to_back(part - 1)
+        to_spectra(part)
+        to_grid(part - 1)
+    to_back(CHUNKS - 1)
+    to_grid(CHUNKS - 1)
 
 
 def layer(scalars, tensors, bands, slots, rows):

time: 316 us -> 320 us (1.013)
  no operation moved by 1% of the time
where the time goes in v4:
time: 320 us; the launch traced here: 317 us
  Pallas kernels  286 us (89%)
  other arithmetic  16.3 us (5%)
  starting transfers between devices  7.35 us (2%)
  local copies, waits for them, and re-layouts  6.37 us (2%)
    pallas_call x1, Pallas kernels, layer(): pl.pallas_call(lambda *refs: layer_kernel(bands, slots, *refs), out_shape...  286 us
    all_to_all x1, starting transfers between devices, per_device(): lax.all_to_all(target_of, 'band', split_axis=0, concat_axis=0, tiled=True)  7.35 us
  transfers between devices with their start and end apart: 1, of which 0 were waited for; matrix products, arithmetic and copies ran while one was open for 4% of the time, Pallas kernels for 0%

profile of v4, /device:TPU:1, one launch (start us, length us, event | category | flops | bytes accessed | tf_op | source)
XLA Modules:
  0.0 316.7 jit_solution(8625203067736026340)
XLA Ops:
  0.7 0.9 convert_reduce_fusion.3
  1.6 0.7 multiply_add_fusion
  2.2 1.4 select_reduce_fusion.3
  3.7 0.7 all_to_all.6
  4.4 7.3 %all-to-all-start = ((s32[16,1,9]{2,1,0:T(1,128)}), s32[16,1,9]{2,1,0:T(1,128)S(1)}, u32[]{:S(2)}, u32[]{:S(2)}) async-start(s32[16,1,9]{2,1,0:T(1,128)} %bitcast.2), calls=%async_computation | async-start | bytes 16384 | tf_op jit(solution)/shard_map/all_to_all | solution.py:428
  11.8 0.7 or_select_fusion
  12.4 0.8 broadcast_in_dim.127
  13.2 0.1 fusion.39
  13.4 0.2 negate_convert_fusion
  13.5 0.1 mul.212
  13.6 1.1 fusion.25
  14.7 2.7 fusion.6
  17.4 1.4 negate_select_fusion.1
  18.8 3.0 negate_select_fusion
  21.8 0.7 fusion.31
  22.5 0.6 dynamic_slice.3.refs_6_
  23.2 0.0 all-to-all-done
  23.2 0.5 broadcast.145
  23.6 0.6 reduce.3
  24.2 0.1 reshape.105
  24.3 0.7 convert_reduce_fusion.1.refs_5_
  25.0 0.1 convert_reduce_fusion.2
  25.1 0.2 convert_reduce_fusion
  25.3 0.5 add_maximum_fusion.refs_4_
  25.8 0.7 select_reduce_fusion
  26.5 0.6 compare_convert_fusion.refs_3_
  27.1 285.9 %layer.1 = bf16[5760,256]{1,0:T(8,128)(2,1)} custom-call(s32[144]{0:T(256)} %get-tuple-element.10.refs_0_, s32[144]{0:T(256)} %get-tuple-element.9.refs_1_, s32[144]{0:T(256)} %get-tuple-element.6.refs_2_, f32[144]{0:T(256)} %compare_convert_fusion.refs_3_, s32[45]{0:T(128)} %add_maximum_fusion.refs_4_, f32[45]{0:T(128)} %convert_reduce_fusion.1.refs_5_, ...), custom_call_target="tpu_custom_call" | custom-call | tf_op jit(solution)/shard_map/layer/pallas_call | solution.py:368
  313.1 3.6 %copy.13 = bf16[5760,256]{1,0:T(8,128)(2,1)} copy(bf16[5760,256]{1,0:T(8,128)(2,1)} %layer.1) | data formatting | bytes 5898240
  (7 shorter events, 0.0 us)
Async XLA Ops:
  4.4 18.8 %all-to-all-start = ((s32[16,1,9]{2,1,0:T(1,128)}), s32[16,1,9]{2,1,0:T(1,128)S(1)}, u32[]{:S(2)}, u32[]{:S(2)}) async-start(s32[16,1,9]{2,1,0:T(1,128)} %bitcast.2), calls=%async_computation | async-start | bytes 16384 | tf_op jit(solution)/shard_map/all_to_all | solution.py:428
